TPU v7x, 32 devices: a whole 2x2x4 slice. The times are simulated.
32 devices in a mesh: dp: 8 (over y, x, core), tensor: 4 (over z).
Axes of the slice: x: 2, y: 2, z: 4, core: 2. Of those that a mesh axis runs over, the one named last changes fastest.
Arguments:
- hidden_in: bfloat16 [4096, 1024], P(('dp', 'tensor')), may hold values from -6 to 6
- norm_in_gain: float32 [1024], replicated, may hold values from 0.5 to 1.5
- query_weight: bfloat16 [1024, 512], P('dp', 'tensor'), may hold values from -0.1875 to 0.1875
- key_weight: bfloat16 [1024, 128], P('dp'), may hold values from -0.1875 to 0.1875
- value_weight: bfloat16 [1024, 128], P('dp'), may hold values from -0.1875 to 0.1875
- output_weight: bfloat16 [512, 1024], P('tensor', 'dp'), may hold values from -2 to 2
- gate_weight: bfloat16 [1024, 1536], P('dp', 'tensor'), may hold values from -0.1875 to 0.1875
- inner_weight: bfloat16 [1024, 1536], P('dp', 'tensor'), may hold values from -0.1875 to 0.1875
- write_weight: bfloat16 [1024, 128], P('dp'), may hold values from -0.1875 to 0.1875
- read_weight: bfloat16 [1024, 128], P('dp'), may hold values from -0.1875 to 0.1875
- step_weight: bfloat16 [1024, 24], P('dp', 'tensor'), may hold values from -0.1875 to 0.1875
- conv_weight: float32 [4, 1536], P(None, 'tensor'), may hold values from -0.5 to 0.5
- conv_bias: float32 [1536], P('tensor'), may hold values from -0.5 to 0.5
- pair_conv_weight: float32 [4, 256], replicated, may hold values from -0.5 to 0.5
- pair_conv_bias: float32 [256], replicated, may hold values from -0.5 to 0.5
- step_bias: float32 [24], P('tensor'), may hold values from -4.5 to -1.5
- decay_log: float32 [24], P('tensor'), may hold values from 0 to 2.77
- skip_gain: float32 [24], P('tensor'), may hold values from 0.5 to 1.5
- state_gain: float32 [1536], P('tensor'), may hold values from 0.5 to 1.5
- state_out_weight: bfloat16 [1536, 1024], P('tensor', 'dp'), may hold values from -0.15625 to 0.15625
- norm_ffn_gain: float32 [1024], replicated, may hold values from 0.5 to 1.5
- feed_gate_weight: bfloat16 [1024, 2048], P('dp', 'tensor'), may hold values from -0.1875 to 0.1875
- feed_up_weight: bfloat16 [1024, 2048], P('dp', 'tensor'), may hold values from -0.1875 to 0.1875
- feed_down_weight: bfloat16 [2048, 1024], P('tensor', 'dp'), may hold values from -0.125 to 0.125
- out_cotangent: bfloat16 [4096, 1024], P(('dp', 'tensor')), may hold values from -6 to 6
Outputs:
- hidden_out: bfloat16 [4096, 1024], P(('dp', 'tensor'))
- gradient_hidden: float32 [4096, 1024], P(('dp', 'tensor'))
- gradient_norm_in_gain: float32 [1024], replicated
- gradient_query_weight: float32 [1024, 512], P('dp', 'tensor')
- gradient_key_weight: float32 [1024, 128], replicated
- gradient_value_weight: float32 [1024, 128], replicated
- gradient_output_weight: float32 [512, 1024], P('tensor', 'dp')
- gradient_gate_weight: float32 [1024, 1536], P('dp', 'tensor')
- gradient_inner_weight: float32 [1024, 1536], P('dp', 'tensor')
- gradient_write_weight: float32 [1024, 128], replicated
- gradient_read_weight: float32 [1024, 128], replicated
- gradient_step_weight: float32 [1024, 24], P('dp', 'tensor')
- gradient_conv_weight: float32 [4, 1536], P(None, 'tensor')
- gradient_conv_bias: float32 [1536], P('tensor')
- gradient_pair_conv_weight: float32 [4, 256], replicated
- gradient_pair_conv_bias: float32 [256], replicated
- gradient_step_bias: float32 [24], P('tensor')
- gradient_decay_log: float32 [24], P('tensor')
- gradient_skip_gain: float32 [24], P('tensor')
- gradient_state_gain: float32 [1536], P('tensor')
- gradient_state_out_weight: float32 [1536, 1024], P('tensor', 'dp')
- gradient_norm_ffn_gain: float32 [1024], replicated
- gradient_feed_gate_weight: float32 [1024, 2048], P('dp', 'tensor')
- gradient_feed_up_weight: float32 [1024, 2048], P('dp', 'tensor')
- gradient_feed_down_weight: float32 [2048, 1024], P('tensor', 'dp')
All inputs are finite; a program needn't handle non-finite values.
Results may differ from a plain program's by a relative error of at most 0.014.
Values may be sent and summed in bfloat16 or wider, within the bound.
No kernel may reach another device: no remote copies, remote signals or barrier semaphores. Data moves between devices by JAX's collectives and lax.ppermute only.
A program may use at most 128 MiB of HBM per device.

v0:
```python
import jax
import jax.numpy as jnp
from jax import lax
from jax.sharding import PartitionSpec as P

QH = 8
KVH = 2
HD = 64
BLOCK = 128


EPS = 1e-05
THETA = 10000.0
HIGHEST = lax.Precision.HIGHEST


def product(left, right):
    return jnp.dot(left, right, preferred_element_type=jnp.float32)


def product_left(left, right):
    return lax.dot_general(
        left, right, (((0,), (0,)), ((), ())), preferred_element_type=jnp.float32
    )


def product_right(left, right):
    return lax.dot_general(
        left, right, (((1,), (1,)), ((), ())), preferred_element_type=jnp.float32
    )


def rounded(values):
    return lax.optimization_barrier(values.astype(jnp.bfloat16)).astype(jnp.float32)


def root_norm(rows, gain):
    scale = lax.rsqrt(jnp.mean(rows * rows, axis=-1, keepdims=True) + EPS)
    return (rows * scale * gain, scale)


def root_norm_back(rows, scale, gain, upstream):
    weighted = upstream * gain
    inner = jnp.sum(weighted * rows, axis=-1, keepdims=True)
    grad_rows = scale * weighted - rows * scale**3 * inner / rows.shape[-1]
    grad_gain = jnp.sum(upstream * rows * scale, axis=0)
    return (grad_rows, grad_gain)


def rotate(values, heads, sign):
    length = values.shape[0]
    shaped = values.reshape(length, heads, -1)
    half = shaped.shape[2] // 2
    freq = THETA ** (-jnp.arange(half, dtype=jnp.float32) / half)
    angle = jnp.arange(length, dtype=jnp.float32)[:, None] * freq[None, :]
    cosine = jnp.cos(angle)[:, None, :]
    sine = sign * jnp.sin(angle)[:, None, :]
    first = shaped[:, :, :half]
    second = shaped[:, :, half:]
    turned = jnp.concatenate(
        [first * cosine - second * sine, second * cosine + first * sine], axis=2
    )
    return turned.reshape(length, -1)


def causal_conv(values, weight, bias):
    taps = weight.shape[0]
    length = values.shape[0]
    padded = jnp.pad(values, ((taps - 1, 0), (0, 0)))
    total = bias[None, :] + jnp.zeros_like(values)
    for tap in range(taps):
        total = total + weight[tap][None, :] * padded[tap : tap + length]
    return total


def state_block(state, block):
    scaled, decay, write_rows, read_rows = block
    size = decay.shape[0]
    running = jnp.cumsum(decay, axis=0)
    lower = jnp.arange(size)[:, None] >= jnp.arange(size)[None, :]
    spread = running[:, None, :] - running[None, :, :]
    weights = jnp.exp(jnp.where(lower[:, :, None], spread, -1e30))
    intersection = jnp.einsum("tn,sn->ts", read_rows, write_rows, precision=HIGHEST)
    inside = jnp.einsum(
        "tsh,shp->thp", intersection[:, :, None] * weights, scaled, precision=HIGHEST
    )
    earlier = jnp.exp(running)[:, :, None] * jnp.einsum(
        "tn,hpn->thp", read_rows, state, precision=HIGHEST
    )
    last = running[-1]
    carry = jnp.exp(last[None, :] - running)
    fresh = jnp.einsum("sh,shp,sn->hpn", carry, scaled, write_rows, precision=HIGHEST)
    return (jnp.exp(last)[:, None, None] * state + fresh, inside + earlier)


def mixer_state(
    inputs,
    writes,
    reads,
    steps_raw,
    gate_z,
    conv_weight,
    conv_bias,
    pair_weight,
    pair_bias,
    step_bias,
    decay_log,
    skip_gain,
):
    length = inputs.shape[0]
    heads = steps_raw.shape[1]
    width = writes.shape[1]
    mixed_inputs = jax.nn.silu(causal_conv(inputs, conv_weight, conv_bias))
    paired = jax.nn.silu(
        causal_conv(jnp.concatenate([writes, reads], axis=1), pair_weight, pair_bias)
    )
    write_rows = paired[:, :width]
    read_rows = paired[:, width:]
    step = jax.nn.softplus(steps_raw + step_bias[None, :])
    decay = step * (-jnp.exp(decay_log))[None, :]
    shaped = mixed_inputs.reshape(length, heads, -1)
    scaled = shaped * step[:, :, None]
    count = length // BLOCK
    blocks = (
        scaled.reshape(count, BLOCK, heads, -1),
        decay.reshape(count, BLOCK, heads),
        write_rows.reshape(count, BLOCK, width),
        read_rows.reshape(count, BLOCK, width),
    )
    start = jnp.zeros((heads, shaped.shape[2], width), jnp.float32)
    final, outputs = lax.scan(jax.checkpoint(state_block), start, blocks)
    result = outputs.reshape(length, heads, -1) + skip_gain[None, :, None] * shaped
    return result.reshape(length, -1) * jax.nn.silu(gate_z)


def body(
    hidden_in,
    norm_in_gain,
    query_weight,
    key_weight,
    value_weight,
    output_weight,
    gate_weight,
    inner_weight,
    write_weight,
    read_weight,
    step_weight,
    conv_weight,
    conv_bias,
    pair_conv_weight,
    pair_conv_bias,
    step_bias,
    decay_log,
    skip_gain,
    state_gain,
    state_out_weight,
    norm_ffn_gain,
    feed_gate_weight,
    feed_up_weight,
    feed_down_weight,
    out_cotangent,
):
    parts = lax.axis_size("tensor")
    place = lax.axis_index("tensor")
    gathered = (
        lax.all_gather(query_weight, "dp", axis=0, tiled=True),
        lax.all_gather(key_weight, "dp", axis=0, tiled=True),
        lax.all_gather(value_weight, "dp", axis=0, tiled=True),
        lax.all_gather(output_weight, "dp", axis=1, tiled=True),
        lax.all_gather(gate_weight, "dp", axis=0, tiled=True),
        lax.all_gather(inner_weight, "dp", axis=0, tiled=True),
        lax.all_gather(write_weight, "dp", axis=0, tiled=True),
        lax.all_gather(read_weight, "dp", axis=0, tiled=True),
        lax.all_gather(step_weight, "dp", axis=0, tiled=True),
        lax.all_gather(state_out_weight, "dp", axis=1, tiled=True),
        lax.all_gather(feed_gate_weight, "dp", axis=0, tiled=True),
        lax.all_gather(feed_up_weight, "dp", axis=0, tiled=True),
        lax.all_gather(feed_down_weight, "dp", axis=1, tiled=True),
    )
    (
        query_full,
        key_full,
        value_full,
        output_full,
        gate_full,
        inner_full,
        write_full,
        read_full,
        step_full,
        state_out_full,
        feed_gate_full,
        feed_up_full,
        feed_down_full,
    ) = gathered
    rows_in = hidden_in.astype(jnp.float32)
    normed, first_scale = root_norm(rows_in, norm_in_gain)
    mixer_rows = lax.all_gather(normed.astype(jnp.bfloat16), "tensor", axis=0, tiled=True)
    length = mixer_rows.shape[0]
    heads_here = query_full.shape[1] // HD
    key_head = place * heads_here // (QH // KVH)
    scale = HD ** (-0.5)
    key_cols = lax.dynamic_slice_in_dim(key_full, key_head * HD, HD, 1)
    value_cols = lax.dynamic_slice_in_dim(value_full, key_head * HD, HD, 1)
    query_low = (
        rotate(product(mixer_rows, query_full), heads_here, 1.0)
        .astype(jnp.bfloat16)
        .reshape(length, heads_here, HD)
    )
    key_low = rotate(product(mixer_rows, key_cols), 1, 1.0).astype(jnp.bfloat16)
    value_low = product(mixer_rows, value_cols).astype(jnp.bfloat16)
    causal = jnp.arange(length)[:, None] >= jnp.arange(length)[None, :]

    def score_rows():
        raw = (
            jnp.einsum("qhd,kd->hqk", query_low, key_low, preferred_element_type=jnp.float32)
            * scale
        )
        return jnp.where(causal[None], raw, -1e30)

    scores = score_rows()
    top = jnp.max(scores, axis=2, keepdims=True)
    exponent = jnp.exp(scores - top)
    total = jnp.sum(exponent, axis=2, keepdims=True)
    log_total = top + jnp.log(total)
    mixed = jnp.einsum(
        "hqk,kd->qhd",
        (exponent / total).astype(jnp.bfloat16),
        value_low,
        preferred_element_type=jnp.float32,
    )
    mixed_low = mixed.reshape(length, -1).astype(jnp.bfloat16)
    gate_raw = product(mixer_rows, gate_full)
    inner_raw = product(mixer_rows, inner_full)
    write_raw = product(mixer_rows, write_full)
    read_raw = product(mixer_rows, read_full)
    step_raw = product(mixer_rows, step_full)
    gated, state_pull = jax.vjp(
        mixer_state,
        inner_raw,
        write_raw,
        read_raw,
        step_raw,
        gate_raw,
        conv_weight,
        conv_bias,
        pair_conv_weight,
        pair_conv_bias,
        step_bias,
        decay_log,
        skip_gain,
    )
    width_all = gated.shape[1] * parts
    power = lax.psum(jnp.sum(gated * gated, axis=1), "tensor")
    state_scale = lax.rsqrt(power / width_all + EPS)[:, None]
    state_low = (gated * state_scale * state_gain).astype(jnp.bfloat16)
    mixer_shard = lax.psum_scatter(
        product(mixed_low, output_full) + product(state_low, state_out_full),
        "tensor",
        scatter_dimension=0,
        tiled=True,
    )
    middle = rows_in + mixer_shard
    second, second_scale = root_norm(middle, norm_ffn_gain)
    feed_rows, cotangent = (
        lax.all_gather(second.astype(jnp.bfloat16), "tensor", axis=0, tiled=True),
        lax.all_gather(out_cotangent, "tensor", axis=0, tiled=True),
    )
    gate_value = product(feed_rows, feed_gate_full)
    up_value = product(feed_rows, feed_up_full)
    sigma = jax.nn.sigmoid(gate_value)
    swish = gate_value * sigma
    active = (swish * up_value).astype(jnp.bfloat16)
    feed_shard = lax.psum_scatter(
        product(active, feed_down_full).astype(jnp.bfloat16),
        "tensor",
        scatter_dimension=0,
        tiled=True,
    ).astype(jnp.float32)
    hidden_out = (middle + feed_shard).astype(jnp.bfloat16)
    back_weights = (
        lax.all_gather(query_weight, "dp", axis=0, tiled=True),
        lax.all_gather(key_weight, "dp", axis=0, tiled=True),
        lax.all_gather(value_weight, "dp", axis=0, tiled=True),
        lax.all_gather(output_weight, "dp", axis=1, tiled=True),
        lax.all_gather(gate_weight, "dp", axis=0, tiled=True),
        lax.all_gather(inner_weight, "dp", axis=0, tiled=True),
        lax.all_gather(write_weight, "dp", axis=0, tiled=True),
        lax.all_gather(read_weight, "dp", axis=0, tiled=True),
        lax.all_gather(step_weight, "dp", axis=0, tiled=True),
        lax.all_gather(state_out_weight, "dp", axis=1, tiled=True),
        lax.all_gather(feed_gate_weight, "dp", axis=0, tiled=True),
        lax.all_gather(feed_up_weight, "dp", axis=0, tiled=True),
        lax.all_gather(feed_down_weight, "dp", axis=1, tiled=True),
    )
    (
        query_full,
        key_full,
        value_full,
        output_full,
        gate_full,
        inner_full,
        write_full,
        read_full,
        step_full,
        state_out_full,
        feed_gate_full,
        feed_up_full,
        feed_down_full,
    ) = back_weights
    key_cols = lax.dynamic_slice_in_dim(key_full, key_head * HD, HD, 1)
    value_cols = lax.dynamic_slice_in_dim(value_full, key_head * HD, HD, 1)
    grad_feed_down = product_left(active, cotangent)
    grad_active = product_right(cotangent, feed_down_full)
    grad_gate = (grad_active * up_value * sigma * (1.0 + gate_value * (1.0 - sigma))).astype(
        jnp.bfloat16
    )
    grad_up = (grad_active * swish).astype(jnp.bfloat16)
    grad_feed_gate = product_left(feed_rows, grad_gate)
    grad_feed_up = product_left(feed_rows, grad_up)
    grad_second = lax.psum_scatter(
        product_right(grad_gate, feed_gate_full) + product_right(grad_up, feed_up_full),
        "tensor",
        scatter_dimension=0,
        tiled=True,
    )
    grad_middle_norm, grad_ffn_gain = root_norm_back(
        middle, second_scale, norm_ffn_gain, grad_second
    )
    grad_middle = out_cotangent.astype(jnp.float32) + grad_middle_norm
    mixer_cot = lax.all_gather(grad_middle.astype(jnp.bfloat16), "tensor", axis=0, tiled=True)
    grad_output = product_left(mixed_low, mixer_cot)
    grad_state_out = product_left(state_low, mixer_cot)
    grad_state = rounded(product_right(mixer_cot, state_out_full))
    weighted = grad_state * state_gain
    inner_sum = lax.psum(jnp.sum(weighted * gated, axis=1), "tensor")
    grad_gated = state_scale * weighted - gated * state_scale**3 * inner_sum[:, None] / width_all
    grad_state_gain = jnp.sum(grad_state * gated * state_scale, axis=0)
    (
        grad_inner_raw,
        grad_write_raw,
        grad_read_raw,
        grad_step_raw,
        grad_gate_raw,
        grad_conv_weight,
        grad_conv_bias,
        grad_pair_weight,
        grad_pair_bias,
        grad_step_bias,
        grad_decay,
        grad_skip,
    ) = state_pull(grad_gated)
    grad_inner_low = grad_inner_raw.astype(jnp.bfloat16)
    grad_write_low = grad_write_raw.astype(jnp.bfloat16)
    grad_read_low = grad_read_raw.astype(jnp.bfloat16)
    grad_step_low = grad_step_raw.astype(jnp.bfloat16)
    grad_gate_low = grad_gate_raw.astype(jnp.bfloat16)
    grad_mixed = (
        product_right(mixer_cot, output_full).astype(jnp.bfloat16).reshape(length, heads_here, HD)
    )
    probs = jnp.exp(score_rows() - log_total)
    grad_probs = jnp.einsum(
        "qhd,kd->hqk", grad_mixed, value_low, preferred_element_type=jnp.float32
    )
    inner_probs = jnp.sum(probs * grad_probs, axis=2, keepdims=True)
    grad_scores = (probs * (grad_probs - inner_probs)).astype(jnp.bfloat16)
    grad_query_rot = (
        jnp.einsum("hqk,kd->qhd", grad_scores, key_low, preferred_element_type=jnp.float32) * scale
    )
    grad_query = rotate(grad_query_rot.reshape(length, -1), heads_here, -1.0).astype(jnp.bfloat16)
    grad_key_rot = (
        jnp.einsum("hqk,qhd->khd", grad_scores, query_low, preferred_element_type=jnp.float32)
        * scale
    )
    grad_key = (
        rotate(grad_key_rot.reshape(length, -1), heads_here, -1.0)
        .astype(jnp.bfloat16)
        .reshape(length, heads_here, HD)
    )
    grad_value = jnp.einsum(
        "hqk,qhd->khd", probs.astype(jnp.bfloat16), grad_mixed, preferred_element_type=jnp.float32
    ).astype(jnp.bfloat16)
    grad_query_weight = product_left(mixer_rows, grad_query)
    grad_key_head = jnp.einsum(
        "ld,lhe->de", mixer_rows, grad_key, preferred_element_type=jnp.float32
    )
    grad_value_head = jnp.einsum(
        "ld,lhe->de", mixer_rows, grad_value, preferred_element_type=jnp.float32
    )
    grad_gate_weight = product_left(mixer_rows, grad_gate_low)
    grad_inner_weight = product_left(mixer_rows, grad_inner_low)
    grad_write_weight = product_left(mixer_rows, grad_write_low)
    grad_read_weight = product_left(mixer_rows, grad_read_low)
    grad_step_weight = product_left(mixer_rows, grad_step_low)
    total_rows = product_right(grad_query, query_full)
    total_rows = total_rows + jnp.einsum(
        "lhe,de->ld", grad_key, key_cols, preferred_element_type=jnp.float32
    )
    total_rows = total_rows + jnp.einsum(
        "lhe,de->ld", grad_value, value_cols, preferred_element_type=jnp.float32
    )
    total_rows = total_rows + product_right(grad_gate_low, gate_full)
    total_rows = total_rows + product_right(grad_inner_low, inner_full)
    total_rows = total_rows + product_right(grad_write_low, write_full)
    total_rows = total_rows + product_right(grad_read_low, read_full)
    grad_first = lax.psum_scatter(
        total_rows + product_right(grad_step_low, step_full),
        "tensor",
        scatter_dimension=0,
        tiled=True,
    )
    grad_rows_norm, grad_in_gain = root_norm_back(rows_in, first_scale, norm_in_gain, grad_first)
    gradient_hidden = grad_middle + grad_rows_norm

    def spread_out(local, axis_dim):
        whole = list(local.shape)
        whole[axis_dim] = whole[axis_dim] * parts
        empty = jnp.zeros(tuple(whole), jnp.float32)
        return lax.dynamic_update_slice_in_dim(
            empty, local, place * local.shape[axis_dim], axis_dim
        )

    def take_back(whole, local, axis_dim):
        return lax.dynamic_slice_in_dim(
            whole, place * local.shape[axis_dim], local.shape[axis_dim], axis_dim
        )

    key_spread = lax.dynamic_update_slice_in_dim(
        jnp.zeros(key_full.shape, jnp.float32), grad_key_head, key_head * HD, 1
    )
    value_spread = lax.dynamic_update_slice_in_dim(
        jnp.zeros(value_full.shape, jnp.float32), grad_value_head, key_head * HD, 1
    )
    split_sums = (
        lax.psum_scatter(grad_query_weight, "dp", scatter_dimension=0, tiled=True),
        lax.psum_scatter(grad_output, "dp", scatter_dimension=1, tiled=True),
        lax.psum_scatter(grad_gate_weight, "dp", scatter_dimension=0, tiled=True),
        lax.psum_scatter(grad_inner_weight, "dp", scatter_dimension=0, tiled=True),
        lax.psum_scatter(grad_step_weight, "dp", scatter_dimension=0, tiled=True),
        lax.psum_scatter(grad_state_out, "dp", scatter_dimension=1, tiled=True),
        lax.psum_scatter(grad_feed_gate, "dp", scatter_dimension=0, tiled=True),
        lax.psum_scatter(grad_feed_up, "dp", scatter_dimension=0, tiled=True),
        lax.psum_scatter(grad_feed_down, "dp", scatter_dimension=1, tiled=True),
    )
    shared = lax.psum(
        (
            grad_in_gain,
            grad_ffn_gain,
            key_spread,
            value_spread,
            grad_write_weight,
            grad_read_weight,
            grad_pair_weight,
            grad_pair_bias,
            spread_out(grad_conv_weight, 1),
            spread_out(grad_conv_bias, 0),
            spread_out(grad_step_bias, 0),
            spread_out(grad_decay, 0),
            spread_out(grad_skip, 0),
            spread_out(grad_state_gain, 0),
        ),
        ("dp", "tensor"),
    )
    return (
        hidden_out,
        gradient_hidden,
        shared[0],
        split_sums[0],
        shared[2],
        shared[3],
        split_sums[1],
        split_sums[2],
        split_sums[3],
        shared[4],
        shared[5],
        split_sums[4],
        take_back(shared[8], grad_conv_weight, 1),
        take_back(shared[9], grad_conv_bias, 0),
        shared[6],
        shared[7],
        take_back(shared[10], grad_step_bias, 0),
        take_back(shared[11], grad_decay, 0),
        take_back(shared[12], grad_skip, 0),
        take_back(shared[13], grad_state_gain, 0),
        split_sums[5],
        shared[1],
        split_sums[6],
        split_sums[7],
        split_sums[8],
    )


def solution(mesh):
    placed = (
        P(("dp", "tensor"), None),
        P(),
        P("dp", "tensor"),
        P("dp", None),
        P("dp", None),
        P("tensor", "dp"),
        P("dp", "tensor"),
        P("dp", "tensor"),
        P("dp", None),
        P("dp", None),
        P("dp", "tensor"),
        P(None, "tensor"),
        P("tensor"),
        P(),
        P(),
        P("tensor"),
        P("tensor"),
        P("tensor"),
        P("tensor"),
        P("tensor", "dp"),
        P(),
        P("dp", "tensor"),
        P("dp", "tensor"),
        P("tensor", "dp"),
        P(("dp", "tensor"), None),
    )
    return jax.shard_map(
        body,
        mesh=mesh,
        in_specs=placed,
        out_specs=(
            P(("dp", "tensor"), None),
            P(("dp", "tensor"), None),
            P(),
            P("dp", "tensor"),
            P(),
            P(),
            P("tensor", "dp"),
            P("dp", "tensor"),
            P("dp", "tensor"),
            P(),
            P(),
            P("dp", "tensor"),
            P(None, "tensor"),
            P("tensor"),
            P(),
            P(),
            P("tensor"),
            P("tensor"),
            P("tensor"),
            P("tensor"),
            P("tensor", "dp"),
            P(),
            P("dp", "tensor"),
            P("dp", "tensor"),
            P("tensor", "dp"),
        ),
        check_vma=False,
    )
```

profile of v0, /device:TPU:0, one launch (start us, length us, event | category | flops | bytes accessed | tf_op | source)
XLA Modules:
  0.0 1053.3 jit_solution(6993946044366497185)
XLA Ops:
  12.3 11.0 %all_gather.66 = bf16[1024,128]{1,0:T(8,128)(2,1)S(1)} all-gather(bf16[128,128]{1,0:T(8,128)(2,1)} %param.32), channel_id=1, replica_groups=mesh['dp'=8,'tensor'=4] {'dp'}, dimensions={0}, use_global_device_ids=true | all-gather | bytes 294912 | tf_op jit(solution)/shard_map/all_gather | solution.py:167
  23.3 10.1 all_gather.67
  33.4 10.3 all_gather.65
  43.7 10.2 all_gather.68
  53.9 8.7 all_gather.69
  62.6 8.5 all_gather.71
  71.2 9.1 all_gather.72
  81.2 9.6 all_gather.70
  90.8 11.2 %all_gather.73 = bf16[1024,384]{1,0:T(8,128)(2,1)} all-gather(bf16[128,384]{1,0:T(8,128)(2,1)S(1)} %copy-done.76), channel_id=1, replica_groups=mesh['dp'=8,'tensor'=4] {'dp'}, dimensions={0}, use_global_device_ids=true | all-gather | bytes 884736 | tf_op jit(solution)/shard_map/all_gather | solution.py:170
  102.0 11.1 %all_gather.74 = bf16[384,1024]{1,0:T(8,128)(2,1)} all-gather(bf16[384,128]{1,0:T(8,128)(2,1)S(1)} %copy-done.77), channel_id=1, replica_groups=mesh['dp'=8,'tensor'=4] {'dp'}, dimensions={1}, use_global_device_ids=true | all-gather | bytes 884736 | tf_op jit(solution)/shard_map/all_gather | solution.py:175
  134.4 49.8 %while.39 = (s32[]{:T(128)}, f32[6,64,128]{2,1,0:T(8,128)S(1)}, f32[4,128,6,64]{1,0,3,2:T(4,128)}, f32[4,6,64,128]{3,2,1,0:T(8,128)}, f32[4,128,6]{2,1,0:T(8,128...) while((s32[]{:T(128)}, f32[6,64,128]{2,1,0:T(8,128)S(1)}, ...), condition=%wide.region_5.6_spmd.clone, body=%wide.region_3.5_spmd.clone.sunk | while | flops 252444672 | bytes 2828041 | solution.py:131
  138.9 6.0 dynamic_update_slice.101
  151.3 6.0 dynamic_update_slice.101
  163.8 6.0 dynamic_update_slice.101
  176.2 6.0 dynamic_update_slice.101
  184.2 2.3 copy.265
  186.6 2.3 copy.170
  188.9 3.5 multiply_reduce_fusion.10
  192.4 12.0 %psum.112 = f32[512]{0:T(512)S(1)} all-reduce(f32[512]{0:T(512)S(1)} %get-tuple-element.611), channel_id=1, replica_groups=mesh['dp'=8,'tensor'=4] {'tensor'}, use_global_device_ids=true, to_apply=%region_7.8 | all-reduce | flops 512 | bytes 4096 | tf_op jit(solution)/shard_map/psum | solution.py:253
  210.0 2.2 convolution_add_fusion.5
  212.8 40.6 %reduce-scatter.14.cloned.1.call-done = f32[128,1024]{1,0:T(8,128)} async-done(((f32[512,1024]{1,0:T(8,128)}), f32[128,1024]{1,0:T(8,128)}) %reduce-scatter.14.cloned.1.call-update) | async-done | bytes 524304 | tf_op jit(solution)/shard_map/reduce_scatter | solution.py:256
  259.5 24.8 %all-gather.10.cloned.1.call-done = bf16[512,1024]{1,0:T(8,128)(2,1)} async-done(((bf16[128,1024]{1,0:T(8,128)(2,1)}), bf16[512,1024]{1,0:T(8,128)(2,1)}) %all-gather.10.cloned.1.call-update) | async-done | bytes 1048592 | tf_op jit(solution)/shard_map/all_gather | solution.py:265
  284.3 3.3 fusion.147
  287.5 21.4 %all-gather.14.cloned.1.call-done = bf16[1024,512]{1,0:T(8,128)(2,1)} async-done(((bf16[128,512]{1,0:T(8,128)(2,1)}), bf16[1024,512]{1,0:T(8,128)(2,1)}) %all-gather.14.cloned.1.call-update) | async-done | bytes 1048592 | tf_op jit(solution)/shard_map/all_gather | solution.py:177
  308.9 3.2 fusion.148
  312.2 26.3 %all-gather.18.cloned.1.call-done = bf16[512,1024]{1,0:T(8,128)(2,1)} async-done(((bf16[128,1024]{1,0:T(8,128)(2,1)}), bf16[512,1024]{1,0:T(8,128)(2,1)}) %all-gather.18.cloned.1.call-update) | async-done | bytes 1048592 | tf_op jit(solution)/shard_map/all_gather | solution.py:266
  338.5 24.9 %all-gather.16.cloned.1.call-done = bf16[512,1024]{1,0:T(8,128)(2,1)} async-done(((bf16[512,128]{1,0:T(8,128)(2,1)}), bf16[512,1024]{1,0:T(8,128)(2,1)}) %all-gather.16.cloned.1.call-update) | async-done | bytes 1048592 | tf_op jit(solution)/shard_map/all_gather | solution.py:178
  363.4 4.2 multiply_convert_fusion
  369.1 2.1 convolution_add_fusion.4
  371.3 3.1 convolution_convert_fusion
  374.5 40.8 %reduce-scatter.18.cloned.1.call-done = f32[128,1024]{1,0:T(8,128)} async-done(((f32[512,1024]{1,0:T(8,128)}), f32[128,1024]{1,0:T(8,128)}) %reduce-scatter.18.cloned.1.call-update) | async-done | bytes 524304 | tf_op jit(solution)/shard_map/reduce_scatter | solution.py:320
  415.3 2.0 multiply_reduce_fusion.11
  417.2 26.7 %reduce-scatter.16.cloned.1.call-done = bf16[128,1024]{1,0:T(8,128)(2,1)} async-done(((bf16[512,1024]{1,0:T(8,128)(2,1)}), bf16[128,1024]{1,0:T(8,128)(2,1)}) %reduce-scatter.16.cloned.1.call-update) | async-done | bytes 262160 | tf_op jit(solution)/shard_map/reduce_scatter | solution.py:273
  443.9 2.7 fusion.135
  447.7 2.3 copy.182
  450.8 22.5 %all-gather.20.cloned.1.call-done = bf16[512,1024]{1,0:T(8,128)(2,1)} async-done(((bf16[128,1024]{1,0:T(8,128)(2,1)}), bf16[512,1024]{1,0:T(8,128)(2,1)}) %all-gather.20.cloned.1.call-update) | async-done | bytes 1048592 | tf_op jit(solution)/shard_map/all_gather | solution.py:330
  481.1 10.1 psum.113
  491.3 3.6 multiply_reduce_fusion.4
  499.5 99.8 %while.40 = (s32[]{:T(128)}, f32[6,64,128]{2,1,0:T(8,128)}, f32[4,128,6,64]{1,0,3,2:T(4,128)}, f32[4,128,6]{2,1,0:T(8,128)}, f32[4,128,128]{2,1,0:T(8,128)}, /*i...) while((s32[]{:T(128)}, f32[6,64,128]{2,1,0:T(8,128)}, ...), condition=%wide.region_27.28_spmd.clone, body=%wide.region_18.27_spmd.clone.sunk | while | flops 606080768 | bytes 7465515 | solution.py:131
  515.0 5.9 dynamic_update_slice.105
  540.1 5.9 dynamic_update_slice.105
  565.3 5.9 dynamic_update_slice.105
  590.4 5.9 dynamic_update_slice.105
  601.5 3.2 multiply_reduce_fusion.14
  621.7 2.2 add_add_fusion
  625.1 3.1 fusion.163
  628.3 3.2 fusion.164
  632.7 3.2 fusion.165
  638.2 2.2 fusion.156
  641.2 3.0 dynamic_update_slice.74
  644.3 2.0 fusion.158
  646.4 2.1 fusion.157
  649.3 3.2 dynamic_update_slice.75
  662.7 3.0 reduce-scatter.20.cloned.1.call-done
  666.9 41.3 %all-reduce.21 = (f32[1024]{0:T(1024)}, f32[4,1536]{1,0:T(4,128)S(1)}, f32[1536]{0:T(1024)S(1)}, f32[4,256]{1,0:T(4,128)}, f32[256]{0:T(256)}, /*index=5*/f32[24...) all-reduce(f32[1024]{0:T(1024)S(1)} %get-tuple-element.535, ...), channel_id=1, replica_groups=mesh['dp'=8,'tensor'=4] {'dp','tensor'}, use_global_device_ids=true, to_apply=%region_32.33 | all-reduce | flops 12616 | bytes 100928 | tf_op jit(solution)/shard_map/psum | solution.py:444
  711.9 2.1 fusion.98
  714.0 42.2 %reduce-scatter.36.cloned.1.call-done = f32[128,512]{1,0:T(8,128)} async-done(((f32[1024,512]{1,0:T(8,128)}), f32[128,512]{1,0:T(8,128)}) %reduce-scatter.36.cloned.1.call-update) | async-done | bytes 262160 | tf_op jit(solution)/shard_map/reduce_scatter | solution.py:441
  756.2 45.2 %reduce-scatter.38.cloned.1.call-done = f32[512,128]{1,0:T(8,128)} async-done(((f32[512,1024]{1,0:T(8,128)}), f32[512,128]{1,0:T(8,128)}) %reduce-scatter.38.cloned.1.call-update) | async-done | bytes 262160 | tf_op jit(solution)/shard_map/reduce_scatter | solution.py:442
  801.4 35.1 %reduce-scatter.30.cloned.1.call-done = f32[128,6]{0,1:T(8,128)} async-done(((f32[1024,6]{0,1:T(8,128)}), f32[128,6]{0,1:T(8,128)}) %reduce-scatter.30.cloned.1.call-update) | async-done | bytes 3088 | tf_op jit(solution)/shard_map/reduce_scatter | solution.py:438
  836.4 38.4 %reduce-scatter.22.cloned.1.call-done = f32[128,128]{1,0:T(8,128)} async-done(((f32[1024,128]{1,0:T(8,128)}), f32[128,128]{1,0:T(8,128)}) %reduce-scatter.22.cloned.1.call-update) | async-done | bytes 65552 | tf_op jit(solution)/shard_map/reduce_scatter | solution.py:434
  874.9 37.7 %reduce-scatter.24.cloned.1.call-done = f32[128,128]{1,0:T(8,128)} async-done(((f32[128,1024]{1,0:T(8,128)}), f32[128,128]{1,0:T(8,128)}) %reduce-scatter.24.cloned.1.call-update) | async-done | bytes 65552 | tf_op jit(solution)/shard_map/reduce_scatter | solution.py:435
  912.6 42.6 %reduce-scatter.32.cloned.1.call-done = f32[384,128]{1,0:T(8,128)} async-done(((f32[384,1024]{1,0:T(8,128)}), f32[384,128]{1,0:T(8,128)}) %reduce-scatter.32.cloned.1.call-update) | async-done | bytes 196624 | tf_op jit(solution)/shard_map/reduce_scatter | solution.py:439
  955.2 42.6 %reduce-scatter.28.cloned.1.call-done = f32[128,384]{1,0:T(8,128)} async-done(((f32[1024,384]{1,0:T(8,128)}), f32[128,384]{1,0:T(8,128)}) %reduce-scatter.28.cloned.1.call-update) | async-done | bytes 196624 | tf_op jit(solution)/shard_map/reduce_scatter | solution.py:437
  997.7 42.6 %reduce-scatter.26.cloned.1.call-done = f32[128,384]{1,0:T(8,128)} async-done(((f32[1024,384]{1,0:T(8,128)}), f32[128,384]{1,0:T(8,128)}) %reduce-scatter.26.cloned.1.call-update) | async-done | bytes 196624 | tf_op jit(solution)/shard_map/reduce_scatter | solution.py:436
  (640 shorter events, 201.0 us)
Async XLA Ops:
  8.0 45.9 %copy-start.131 = (bf16[128,6]{0,1:T(8,128)(2,1)S(1)}, bf16[128,6]{0,1:T(8,128)(2,1)}, u32[]{:S(2)}) copy-start(bf16[128,6]{0,1:T(8,128)(2,1)} %param.39) | copy-start | bytes 4612
  8.0 54.5 %copy-start.88 = (bf16[128,128]{1,0:T(8,128)(2,1)S(1)}, bf16[128,128]{1,0:T(8,128)(2,1)}, u32[]{:S(2)}) copy-start(bf16[128,128]{1,0:T(8,128)(2,1)} %param.37) | copy-start | bytes 98308
  8.1 63.0 %copy-start.136 = (f32[6]{0:T(128)S(1)}, f32[6]{0:T(128)}, u32[]{:S(2)}) copy-start(f32[6]{0:T(128)} %param.46) | copy-start | bytes 76
  8.1 63.2 %copy-start.89 = (bf16[128,128]{1,0:T(8,128)(2,1)S(1)}, bf16[128,128]{1,0:T(8,128)(2,1)}, u32[]{:S(2)}) copy-start(bf16[128,128]{1,0:T(8,128)(2,1)} %param.38) | copy-start | bytes 98308
  8.1 72.3 %copy-start.118 = (f32[4,384]{1,0:T(4,128)S(1)}, f32[4,384]{1,0:T(4,128)}, u32[]{:S(2)}) copy-start(f32[4,384]{1,0:T(4,128)} %param.40) | copy-start | bytes 18436
  8.1 73.1 %copy-start.75 = (bf16[128,384]{1,0:T(8,128)(2,1)S(1)}, bf16[128,384]{1,0:T(8,128)(2,1)}, u32[]{:S(2)}) copy-start(bf16[128,384]{1,0:T(8,128)(2,1)} %param.36) | copy-start | bytes 294916
  8.1 82.7 %copy-start.76 = (bf16[128,384]{1,0:T(8,128)(2,1)S(1)}, bf16[128,384]{1,0:T(8,128)(2,1)}, u32[]{:S(2)}) copy-start(bf16[128,384]{1,0:T(8,128)(2,1)} %param.35) | copy-start | bytes 294916
  8.1 106.1 %all-gather.8.cloned.1.call-start = ((), (), s32[]{:S(2)}) async-start(), calls=%async_computation.13 | async-start | bytes 1310720 | tf_op jit(solution)/shard_map/all_gather | solution.py:197
  12.2 89.8 %copy-start.77 = (bf16[384,128]{1,0:T(8,128)(2,1)S(1)}, bf16[384,128]{1,0:T(8,128)(2,1)}, u32[]{:S(2)}) copy-start(bf16[384,128]{1,0:T(8,128)(2,1)} %param.48) | copy-start | bytes 294916
  12.2 241.2 %reduce-scatter.14.cloned.1.call-start = ((), (), s32[]{:S(2)}) async-start(), calls=%async_computation.14 | async-start | bytes 2621440 | tf_op jit(solution)/shard_map/reduce_scatter | solution.py:256
  23.3 90.9 %copy-start.43 = (bf16[1024,128]{1,0:T(8,128)(2,1)}, bf16[1024,128]{1,0:T(8,128)(2,1)S(1)}, u32[]{:S(2)}) copy-start(bf16[1024,128]{1,0:T(8,128)(2,1)S(1)} %all_gather.66) | copy-start | bytes 786436
  33.4 79.7 %copy-start.137 = (f32[6]{0:T(128)S(1)}, f32[6]{0:T(128)}, u32[]{:S(2)}) copy-start(f32[6]{0:T(128)} %param.45) | copy-start | bytes 76
  33.4 79.7 %copy-start.127 = (f32[4,256]{1,0:T(4,128)S(1)}, f32[4,256]{1,0:T(4,128)}, u32[]{:S(2)}) copy-start(f32[4,256]{1,0:T(4,128)} %param.42) | copy-start | bytes 12292
  62.6 60.6 %copy-start.69 = (bf16[1024,6]{0,1:T(8,128)(2,1)}, bf16[1024,6]{0,1:T(8,128)(2,1)S(1)}, u32[]{:S(2)}) copy-start(bf16[1024,6]{0,1:T(8,128)(2,1)S(1)} %all_gather.69) | copy-start | bytes 36868
  71.1 54.5 %copy-start.31 = (bf16[1024,128]{1,0:T(8,128)(2,1)}, bf16[1024,128]{1,0:T(8,128)(2,1)S(1)}, u32[]{:S(2)}) copy-start(bf16[1024,128]{1,0:T(8,128)(2,1)S(1)} %all_gather.71) | copy-start | bytes 786436
  71.2 117.6 %copy-start.90 = (f32[384]{0:T(512)}, f32[384]{0:T(512)S(1)}, u32[]{:S(2)}) copy-start(f32[384]{0:T(512)S(1)} %mul.1037) | copy-start | bytes 4612
  80.3 45.8 %copy-start.33 = (bf16[1024,128]{1,0:T(8,128)(2,1)}, bf16[1024,128]{1,0:T(8,128)(2,1)S(1)}, u32[]{:S(2)}) copy-start(bf16[1024,128]{1,0:T(8,128)(2,1)S(1)} %all_gather.72) | copy-start | bytes 786436
  80.4 38.5 %copy-start.93 = (f32[384]{0:T(512)}, f32[384]{0:T(512)S(1)}, u32[]{:S(2)}) copy-start(f32[384]{0:T(512)S(1)} %get-tuple-element.539) | copy-start | bytes 4612
  80.4 38.5 %copy-start.95 = (f32[384]{0:T(512)}, f32[384]{0:T(512)S(1)}, u32[]{:S(2)}) copy-start(f32[384]{0:T(512)S(1)} %get-tuple-element.540) | copy-start | bytes 4612
  80.4 38.5 %copy-start.97 = (f32[384]{0:T(512)}, f32[384]{0:T(512)S(1)}, u32[]{:S(2)}) copy-start(f32[384]{0:T(512)S(1)} %get-tuple-element.541) | copy-start | bytes 4612
  80.4 38.5 %copy-start.99 = (f32[384]{0:T(512)}, f32[384]{0:T(512)S(1)}, u32[]{:S(2)}) copy-start(f32[384]{0:T(512)S(1)} %get-tuple-element.542) | copy-start | bytes 4612
  90.8 28.0 %copy-start.11 = (bf16[1024,384]{1,0:T(8,128)(2,1)}, bf16[1024,384]{1,0:T(8,128)(2,1)S(1)}, u32[]{:S(2)}) copy-start(bf16[1024,384]{1,0:T(8,128)(2,1)S(1)} %all_gather.70) | copy-start | bytes 2359300
  113.1 10.1 copy-start.128
  113.2 13.7 %copy-start.104 = (f32[1,256]{1,0:T(1,128)}, f32[1,256]{1,0:T(1,128)S(1)}, u32[]{:S(2)}) copy-start(f32[1,256]{1,0:T(1,128)S(1)} %get-tuple-element.655) | copy-start | bytes 3076
  113.2 13.7 %copy-start.106 = (f32[1,256]{1,0:T(1,128)}, f32[1,256]{1,0:T(1,128)S(1)}, u32[]{:S(2)}) copy-start(f32[1,256]{1,0:T(1,128)S(1)} %get-tuple-element.656) | copy-start | bytes 3076
  113.2 13.7 %copy-start.108 = (f32[1,256]{1,0:T(1,128)}, f32[1,256]{1,0:T(1,128)S(1)}, u32[]{:S(2)}) copy-start(f32[1,256]{1,0:T(1,128)S(1)} %get-tuple-element.657) | copy-start | bytes 3076
  113.2 13.7 %copy-start.110 = (f32[1,256]{1,0:T(1,128)}, f32[1,256]{1,0:T(1,128)S(1)}, u32[]{:S(2)}) copy-start(f32[1,256]{1,0:T(1,128)S(1)} %get-tuple-element.658) | copy-start | bytes 3076
  114.2 91.3 %copy-start.58 = (f32[512,32]{0,1:T(8,128)}, f32[512,32]{0,1:T(8,128)S(1)}, u32[]{:S(2)}) copy-start(f32[512,32]{0,1:T(8,128)S(1)} %get-tuple-element.665) | copy-start | bytes 196612
  120.3 68.6 %copy-start.15 = (f32[512,384]{1,0:T(8,128)}, f32[512,384]{1,0:T(8,128)S(1)}, u32[]{:S(2)}) copy-start(f32[512,384]{1,0:T(8,128)S(1)} %get-tuple-element.616) | copy-start | bytes 2359300
  188.9 16.1 %copy-start.35 = (bf16[1024,128]{1,0:T(8,128)(2,1)S(1)}, bf16[1024,128]{1,0:T(8,128)(2,1)}, u32[]{:S(2)}) copy-start(bf16[1024,128]{1,0:T(8,128)(2,1)} %all_gather.67) | copy-start | bytes 786436
  188.9 16.6 %copy-start.68 = (f32[512,32]{0,1:T(8,128)S(1)}, f32[512,32]{0,1:T(8,128)}, u32[]{:S(2)}) copy-start(f32[512,32]{0,1:T(8,128)} %get-tuple-element.664) | copy-start | bytes 196612
  192.4 13.2 %copy-start.71 = (bf16[512,1,32]{0,2,1:T(8,128)(2,1)S(1)}, bf16[512,1,32]{0,2,1:T(8,128)(2,1)}, u32[]{:S(2)}) copy-start(bf16[512,1,32]{0,2,1:T(8,128)(2,1)} %get-tuple-element.648) | copy-start | bytes 98308
  192.4 13.2 %copy-start.73 = (bf16[512,1,32]{0,2,1:T(8,128)(2,1)S(1)}, bf16[512,1,32]{0,2,1:T(8,128)(2,1)}, u32[]{:S(2)}) copy-start(bf16[512,1,32]{0,2,1:T(8,128)(2,1)} %get-tuple-element.649) | copy-start | bytes 98308
  212.2 41.3 %copy-start.20 = (bf16[128,1024]{1,0:T(8,128)(2,1)S(1)}, bf16[128,1024]{1,0:T(8,128)(2,1)}, u32[]{:S(2)}) copy-start(bf16[128,1024]{1,0:T(8,128)(2,1)} %param.29) | copy-start | bytes 786436
  212.2 47.3 %all-gather.12.cloned.1.call-start = ((), (), s32[]{:S(2)}) async-start(), calls=%async_computation.16 | async-start | bytes 1179648 | tf_op jit(solution)/shard_map/all_gather | solution.py:176
  212.8 71.5 %all-gather.10.cloned.1.call-start = ((), (), s32[]{:S(2)}) async-start(), calls=%async_computation.15 | async-start | bytes 1310720 | tf_op jit(solution)/shard_map/all_gather | solution.py:265
  255.2 160.1 %copy-start.119 = (f32[128]{0:T(128)}, f32[128]{0:T(128)S(1)}, u32[]{:S(2)}) copy-start(f32[128]{0:T(128)S(1)} %get-tuple-element.667) | copy-start | bytes 1540
  257.0 52.0 %all-gather.14.cloned.1.call-start = ((), (), s32[]{:S(2)}) async-start(), calls=%async_computation.17 | async-start | bytes 1179648 | tf_op jit(solution)/shard_map/all_gather | solution.py:177
  257.5 81.0 %all-gather.18.cloned.1.call-start = ((), (), s32[]{:S(2)}) async-start(), calls=%async_computation.20 | async-start | bytes 1310720 | tf_op jit(solution)/shard_map/all_gather | solution.py:266
  258.3 105.1 %all-gather.16.cloned.1.call-start = ((), (), s32[]{:S(2)}) async-start(), calls=%async_computation.18 | async-start | bytes 1179648 | tf_op jit(solution)/shard_map/all_gather | solution.py:178
  259.0 156.2 %reduce-scatter.18.cloned.1.call-start = ((), (), s32[]{:S(2)}) async-start(), calls=%async_computation.21 | async-start | bytes 2621440 | tf_op jit(solution)/shard_map/reduce_scatter | solution.py:320
  371.2 44.0 %copy-start.83 = (f32[1024]{0:T(1024)S(1)}, f32[1024]{0:T(1024)}, u32[]{:S(2)}) copy-start(f32[1024]{0:T(1024)} %param.49) | copy-start | bytes 12292
  371.3 72.7 %reduce-scatter.16.cloned.1.call-start = ((), (), s32[]{:S(2)}) async-start(), calls=%async_computation.19 | async-start | bytes 1310720 | tf_op jit(solution)/shard_map/reduce_scatter | solution.py:273
  374.4 98.9 %all-gather.20.cloned.1.call-start = ((), (), s32[]{:S(2)}) async-start(), calls=%async_computation.22 | async-start | bytes 1310720 | tf_op jit(solution)/shard_map/all_gather | solution.py:330
  443.9 29.4 %copy-start.38 = (bf16[128,1024]{1,0:T(8,128)(2,1)S(1)}, bf16[128,1024]{1,0:T(8,128)(2,1)}, u32[]{:S(2)}) copy-start(bf16[128,1024]{1,0:T(8,128)(2,1)} %all_gather.68) | copy-start | bytes 786436
  446.6 219.0 %reduce-scatter.20.cloned.1.call-start = ((), (), s32[]{:S(2)}) async-start(), calls=%async_computation.23 | async-start | bytes 2621440 | tf_op jit(solution)/shard_map/reduce_scatter | solution.py:405
  479.5 11.8 %copy-start.3 = (f32[512,384]{1,0:T(8,128)S(1)}, f32[512,384]{1,0:T(8,128)}, u32[]{:S(2)}) copy-start(f32[512,384]{1,0:T(8,128)} %get-tuple-element.612) | copy-start | bytes 2359300
  479.5 11.8 %copy-start.16 = (f32[512,384]{1,0:T(8,128)S(1)}, f32[512,384]{1,0:T(8,128)}, u32[]{:S(2)}) copy-start(f32[512,384]{1,0:T(8,128)} %copy-done.15) | copy-start | bytes 2359300
  479.5 11.8 %copy-start.91 = (f32[384]{0:T(512)S(1)}, f32[384]{0:T(512)}, u32[]{:S(2)}) copy-start(f32[384]{0:T(512)} %copy-done.90) | copy-start | bytes 4612
  479.5 11.8 %copy-start.113 = (f32[512]{0:T(512)S(1)}, f32[512]{0:T(512)}, u32[]{:S(2)}) copy-start(f32[512]{0:T(512)} %get-tuple-element.659) | copy-start | bytes 6148
  623.9 90.1 %reduce-scatter.34.cloned.1.call-start = ((), (), s32[]{:S(2)}) async-start(), calls=%async_computation.30 | async-start | bytes 2359296 | tf_op jit(solution)/shard_map/reduce_scatter | solution.py:440
  628.3 127.9 %reduce-scatter.36.cloned.1.call-start = ((), (), s32[]{:S(2)}) async-start(), calls=%async_computation.31 | async-start | bytes 2359296 | tf_op jit(solution)/shard_map/reduce_scatter | solution.py:441
  631.5 169.9 %reduce-scatter.38.cloned.1.call-start = ((), (), s32[]{:S(2)}) async-start(), calls=%async_computation.32 | async-start | bytes 2359296 | tf_op jit(solution)/shard_map/reduce_scatter | solution.py:442
  635.9 200.5 %reduce-scatter.30.cloned.1.call-start = ((), (), s32[]{:S(2)}) async-start(), calls=%async_computation.28 | async-start | bytes 36864 | tf_op jit(solution)/shard_map/reduce_scatter | solution.py:438
  636.8 238.0 %reduce-scatter.22.cloned.1.call-start = ((), (), s32[]{:S(2)}) async-start(), calls=%async_computation.24 | async-start | bytes 589824 | tf_op jit(solution)/shard_map/reduce_scatter | solution.py:434
  638.2 274.4 %reduce-scatter.24.cloned.1.call-start = ((), (), s32[]{:S(2)}) async-start(), calls=%async_computation.25 | async-start | bytes 589824 | tf_op jit(solution)/shard_map/reduce_scatter | solution.py:435
  646.3 266.3 %all-reduce.25.cloned.1.call-start = ((), (), s32[]{:S(2)}) async-start(), calls=%async_computation.33 | async-start | bytes 4194304 | tf_op jit(solution)/shard_map/psum | solution.py:444
  655.0 300.1 %reduce-scatter.32.cloned.1.call-start = ((), (), s32[]{:S(2)}) async-start(), calls=%async_computation.29 | async-start | bytes 1769472 | tf_op jit(solution)/shard_map/reduce_scatter | solution.py:439
  657.0 340.7 %reduce-scatter.28.cloned.1.call-start = ((), (), s32[]{:S(2)}) async-start(), calls=%async_computation.27 | async-start | bytes 1769472 | tf_op jit(solution)/shard_map/reduce_scatter | solution.py:437
  659.2 52.7 %copy-start.49 = (f32[128,1024]{1,0:T(8,128)S(1)}, f32[128,1024]{1,0:T(8,128)}, u32[]{:S(2)}) copy-start(f32[128,1024]{1,0:T(8,128)} %get-tuple-element.608) | copy-start | bytes 1572868
  659.2 52.7 %copy-start.139 = (f32[128]{0:T(128)S(1)}, f32[128]{0:T(128)}, u32[]{:S(2)}) copy-start(f32[128]{0:T(128)} %get-tuple-element.661) | copy-start | bytes 1540
  659.2 381.1 %reduce-scatter.26.cloned.1.call-start = ((), (), s32[]{:S(2)}) async-start(), calls=%async_computation.26 | async-start | bytes 1769472 | tf_op jit(solution)/shard_map/reduce_scatter | solution.py:436
  912.6 131.5 %copy-start.63 = (f32[1024,128]{1,0:T(8,128)S(1)}, f32[1024,128]{1,0:T(8,128)}, u32[]{:S(2)}) copy-start(f32[1024,128]{1,0:T(8,128)} %get-tuple-element.938) | copy-start | bytes 1572868
  912.6 132.3 %copy-start.62 = (f32[1024,128]{1,0:T(8,128)S(1)}, f32[1024,128]{1,0:T(8,128)}, u32[]{:S(2)}) copy-start(f32[1024,128]{1,0:T(8,128)} %get-tuple-element.939) | copy-start | bytes 1572868
  (100 other events, 246.0 us)
Sparse Core Ops, SparseCore 0:
  12.3 30.6 all-gather.7
  212.3 41.0 reduce-scatter.13
  371.4 43.8 reduce-scatter.17
  417.4 26.4 reduce-scatter.15
  655.2 142.4 all-reduce.24
Sparse Core Ops, SparseCore 1:
  214.7 20.5 all-gather.11
  257.0 27.2 all-gather.9
  286.2 22.7 all-gather.13
  310.6 27.8 all-gather.17
  340.6 22.8 all-gather.15
  446.7 26.5 all-gather.19
  624.0 41.6 reduce-scatter.19
  669.4 41.2 reduce-scatter.33
  714.8 41.4 reduce-scatter.35
  760.1 41.3 reduce-scatter.37
  805.1 31.3 reduce-scatter.29
  840.7 34.1 reduce-scatter.21
  878.4 34.1 reduce-scatter.23
  916.8 38.3 reduce-scatter.31
  959.4 38.3 reduce-scatter.27
  1002.0 38.3 reduce-scatter.25
where the time goes:
time: 1060 us; the launch traced here: 1050 us
  waiting for transfers between devices  560 us (53%)
  blocking collectives  163 us (15%)
  local copies, waits for them, and re-layouts  130 us (12%)
  matrix products  126 us (12%)
  other arithmetic  55 us (5%)
  between operations  17.5 us (2%)
    dynamic_update_slice x12, local copies, waits for them, and re-layouts, mixer_state(): final, outputs = lax.scan(jax.checkpoint(state_block), start, blocks)  50.1 us
    reduce_scatter x1, waiting for transfers between devices, body(): lax.psum_scatter(grad_feed_down, 'dp', scatter_dimension=1, tiled=True)  45.2 us
    reduce_scatter x1, waiting for transfers between devices, body(): lax.psum_scatter(grad_gate_weight, 'dp', scatter_dimension=0, tiled=True)  42.6 us
    reduce_scatter x1, waiting for transfers between devices, body(): lax.psum_scatter(grad_inner_weight, 'dp', scatter_dimension=0, tiled=True)  42.6 us
    reduce_scatter x1, waiting for transfers between devices, body(): lax.psum_scatter(grad_state_out, 'dp', scatter_dimension=1, tiled=True)  42.6 us
    reduce_scatter x1, waiting for transfers between devices, body(): lax.psum_scatter(grad_feed_up, 'dp', scatter_dimension=0, tiled=True)  42.2 us
    psum x1, blocking collectives, body(): lax.psum((grad_in_gain, grad_ffn_gain, key_spread, value_spread, grad_wri...  41.3 us
    reduce_scatter x1, waiting for transfers between devices, body(): lax.psum_scatter(product_right(grad_gate, feed_gate_full) + product_right...  40.8 us
  transfers between devices with their start and end apart: 21, of which 17 were waited for; matrix products, arithmetic and copies ran while one was open for 6% of the time, Pallas kernels for 0%

commit v1 on v0

v1 whole, which is shorter than its diff:
```python
import jax
import jax.numpy as jnp
from jax import lax
from jax.sharding import PartitionSpec as P

QH = 8
KVH = 2
HD = 64
BLOCK = 128


EPS = 1e-05
THETA = 10000.0
HIGHEST = lax.Precision.HIGHEST


def product(left, right):
    return jnp.dot(left, right, preferred_element_type=jnp.float32)


def product_left(left, right):
    return lax.dot_general(
        left, right, (((0,), (0,)), ((), ())), preferred_element_type=jnp.float32
    )


def product_right(left, right):
    return lax.dot_general(
        left, right, (((1,), (1,)), ((), ())), preferred_element_type=jnp.float32
    )


def rounded(values):
    return lax.optimization_barrier(values.astype(jnp.bfloat16)).astype(jnp.float32)


def root_norm(rows, gain):
    scale = lax.rsqrt(jnp.mean(rows * rows, axis=-1, keepdims=True) + EPS)
    return (rows * scale * gain, scale)


def root_norm_back(rows, scale, gain, upstream):
    weighted = upstream * gain
    inner = jnp.sum(weighted * rows, axis=-1, keepdims=True)
    grad_rows = scale * weighted - rows * scale**3 * inner / rows.shape[-1]
    grad_gain = jnp.sum(upstream * rows * scale, axis=0)
    return (grad_rows, grad_gain)


def rotate(values, heads, sign):
    length = values.shape[0]
    shaped = values.reshape(length, heads, -1)
    half = shaped.shape[2] // 2
    freq = THETA ** (-jnp.arange(half, dtype=jnp.float32) / half)
    angle = jnp.arange(length, dtype=jnp.float32)[:, None] * freq[None, :]
    cosine = jnp.cos(angle)[:, None, :]
    sine = sign * jnp.sin(angle)[:, None, :]
    first = shaped[:, :, :half]
    second = shaped[:, :, half:]
    turned = jnp.concatenate(
        [first * cosine - second * sine, second * cosine + first * sine], axis=2
    )
    return turned.reshape(length, -1)


def causal_conv(values, weight, bias):
    taps = weight.shape[0]
    length = values.shape[0]
    padded = jnp.pad(values, ((taps - 1, 0), (0, 0)))
    total = bias[None, :] + jnp.zeros_like(values)
    for tap in range(taps):
        total = total + weight[tap][None, :] * padded[tap : tap + length]
    return total


def state_block(state, block):
    scaled, decay, write_rows, read_rows = block
    size = decay.shape[0]
    running = jnp.cumsum(decay, axis=0)
    lower = jnp.arange(size)[:, None] >= jnp.arange(size)[None, :]
    spread = running[:, None, :] - running[None, :, :]
    weights = jnp.exp(jnp.where(lower[:, :, None], spread, -1e30))
    intersection = jnp.einsum("tn,sn->ts", read_rows, write_rows, precision=HIGHEST)
    inside = jnp.einsum(
        "tsh,shp->thp", intersection[:, :, None] * weights, scaled, precision=HIGHEST
    )
    earlier = jnp.exp(running)[:, :, None] * jnp.einsum(
        "tn,hpn->thp", read_rows, state, precision=HIGHEST
    )
    last = running[-1]
    carry = jnp.exp(last[None, :] - running)
    fresh = jnp.einsum("sh,shp,sn->hpn", carry, scaled, write_rows, precision=HIGHEST)
    return (jnp.exp(last)[:, None, None] * state + fresh, inside + earlier)


def mixer_state(
    inputs,
    writes,
    reads,
    steps_raw,
    gate_z,
    conv_weight,
    conv_bias,
    pair_weight,
    pair_bias,
    step_bias,
    decay_log,
    skip_gain,
):
    length = inputs.shape[0]
    heads = steps_raw.shape[1]
    width = writes.shape[1]
    mixed_inputs = jax.nn.silu(causal_conv(inputs, conv_weight, conv_bias))
    paired = jax.nn.silu(
        causal_conv(jnp.concatenate([writes, reads], axis=1), pair_weight, pair_bias)
    )
    write_rows = paired[:, :width]
    read_rows = paired[:, width:]
    step = jax.nn.softplus(steps_raw + step_bias[None, :])
    decay = step * (-jnp.exp(decay_log))[None, :]
    shaped = mixed_inputs.reshape(length, heads, -1)
    scaled = shaped * step[:, :, None]
    count = length // BLOCK
    blocks = (
        scaled.reshape(count, BLOCK, heads, -1),
        decay.reshape(count, BLOCK, heads),
        write_rows.reshape(count, BLOCK, width),
        read_rows.reshape(count, BLOCK, width),
    )
    start = jnp.zeros((heads, shaped.shape[2], width), jnp.float32)
    final, outputs = lax.scan(jax.checkpoint(state_block), start, blocks)
    result = outputs.reshape(length, heads, -1) + skip_gain[None, :, None] * shaped
    return result.reshape(length, -1) * jax.nn.silu(gate_z)


def swap(values, axis, mask):
    size = lax.axis_size(axis)
    return lax.ppermute(values, axis, [(index, index ^ mask) for index in range(size)])


def tensor_gather(block):
    return [block] + [swap(block, "tensor", mask) for mask in range(1, lax.axis_size("tensor"))]


def paired_sum(terms):
    while len(terms) > 1:
        terms = [terms[at] + terms[at + 1] for at in range(0, len(terms), 2)]
    return terms[0]


def tensor_scatter(blocks):
    got = [
        swap(block.astype(jnp.bfloat16), "tensor", mask).astype(jnp.float32)
        for mask, block in enumerate(blocks)
        if mask
    ]
    return paired_sum([blocks[0]] + got)


def tensor_sum(values):
    return paired_sum(tensor_gather(values))


def in_order(slots, place):
    stacked = jnp.stack(slots)
    parts = len(slots)
    return jnp.concatenate(
        [lax.dynamic_index_in_dim(stacked, place ^ at, 0, keepdims=False) for at in range(parts)]
    )


def dp_gather(block):
    size = lax.axis_size("dp")
    if size != 8:
        return lax.all_gather(block, "dp", axis=0, tiled=True)
    me = lax.axis_index("dp")
    rows = block.shape[0]
    mine = [block] + [swap(block, "dp", 2 * chip) for chip in range(1, size // 2)]
    near = swap(block, "dp", 1)
    far = swap(jnp.stack(mine[1:]), "dp", 1)
    pieces = [(0, block), (1, near)]
    for chip in range(1, size // 2):
        pieces += [(2 * chip, mine[chip]), (2 * chip + 1, far[chip - 1])]
    whole = jnp.zeros((size * rows,) + block.shape[1:], block.dtype)
    for mask, piece in pieces:
        whole = lax.dynamic_update_slice_in_dim(whole, piece, (me ^ mask) * rows, 0)
    return whole


def dp_scatter(whole):
    size = lax.axis_size("dp")
    if size != 8:
        return lax.psum_scatter(whole, "dp", scatter_dimension=0, tiled=True)
    me = lax.axis_index("dp")
    chips = size // 2
    rows = whole.shape[0] // size
    shaped = whole.reshape(chips, 2, rows, whole.shape[1])
    core = me % 2
    chip = me // 2
    keep = lax.dynamic_index_in_dim(shaped, core, 1, keepdims=False)
    give = lax.dynamic_index_in_dim(shaped, 1 - core, 1, keepdims=False)
    low = jnp.bfloat16
    both = keep.astype(jnp.float32) + swap(give.astype(low), "dp", 1).astype(jnp.float32)
    terms = [lax.dynamic_index_in_dim(both, chip, 0, keepdims=False)]
    for mask in range(1, chips):
        part = lax.dynamic_index_in_dim(both, chip ^ mask, 0, keepdims=False).astype(low)
        terms.append(swap(part, "dp", 2 * mask).astype(jnp.float32))
    return paired_sum(terms)


def dp_sum(values):
    size = lax.axis_size("dp")
    if size != 8:
        return lax.psum(values, "dp")
    both = values + swap(values, "dp", 1)
    return paired_sum([both] + [swap(both, "dp", 2 * chip) for chip in range(1, size // 2)])


def body(
    hidden_in,
    norm_in_gain,
    query_weight,
    key_weight,
    value_weight,
    output_weight,
    gate_weight,
    inner_weight,
    write_weight,
    read_weight,
    step_weight,
    conv_weight,
    conv_bias,
    pair_conv_weight,
    pair_conv_bias,
    step_bias,
    decay_log,
    skip_gain,
    state_gain,
    state_out_weight,
    norm_ffn_gain,
    feed_gate_weight,
    feed_up_weight,
    feed_down_weight,
    out_cotangent,
):
    low = jnp.bfloat16
    parts = lax.axis_size("tensor")
    place = lax.axis_index("tensor")
    heads_here = query_weight.shape[1] // HD
    key_head = place * heads_here // (QH // KVH)
    heads_state = step_weight.shape[1]
    width = gate_weight.shape[1]
    units = feed_gate_weight.shape[1]
    scale = HD ** (-0.5)

    mixer_local = jnp.concatenate(
        [
            query_weight,
            lax.dynamic_slice_in_dim(key_weight, key_head * HD, HD, 1),
            lax.dynamic_slice_in_dim(value_weight, key_head * HD, HD, 1),
            write_weight,
            read_weight,
            gate_weight,
            inner_weight,
            jnp.pad(step_weight, ((0, 0), (0, 128 - heads_state))),
        ],
        axis=1,
    )
    late_local = jnp.concatenate(
        [output_weight.T, state_out_weight.T, feed_gate_weight, feed_up_weight, feed_down_weight.T],
        axis=1,
    )
    rows_in = hidden_in.astype(jnp.float32)
    normed, first_scale = root_norm(rows_in, norm_in_gain)
    normed_slots = tensor_gather(normed.astype(low))
    mixer_full = dp_gather(mixer_local)
    late_full = lax.all_gather(late_local, "dp", axis=0, tiled=True)
    out_full = late_full[:, : 128 + width]
    feed_full = late_full[:, 128 + width : 128 + width + 2 * units]
    down_full = late_full[:, 128 + width + 2 * units :]
    mixer_rows = in_order(normed_slots, place)
    length = mixer_rows.shape[0]

    raw = product(mixer_rows, mixer_full)
    raw, cot_block = lax.optimization_barrier((raw, out_cotangent))
    cot_slots = tensor_gather(cot_block)
    query_low = rotate(raw[:, :128], heads_here, 1.0).astype(low).reshape(length, heads_here, HD)
    key_low = rotate(raw[:, 128:192], 1, 1.0).astype(low)
    value_low = raw[:, 192:256].astype(low)
    write_raw = raw[:, 256:384]
    read_raw = raw[:, 384:512]
    gate_raw = raw[:, 512 : 512 + width]
    inner_raw = raw[:, 512 + width : 512 + 2 * width]
    step_raw = raw[:, 512 + 2 * width : 512 + 2 * width + heads_state]

    gated, state_pull = jax.vjp(
        mixer_state,
        inner_raw,
        write_raw,
        read_raw,
        step_raw,
        gate_raw,
        conv_weight,
        conv_bias,
        pair_conv_weight,
        pair_conv_bias,
        step_bias,
        decay_log,
        skip_gain,
    )
    width_all = width * parts
    power = tensor_sum(jnp.sum(gated * gated, axis=1))

    causal = jnp.arange(length)[:, None] >= jnp.arange(length)[None, :]

    def score_rows():
        raw_scores = (
            jnp.einsum("qhd,kd->hqk", query_low, key_low, preferred_element_type=jnp.float32)
            * scale
        )
        return jnp.where(causal[None], raw_scores, -1e30)

    scores = score_rows()
    top = jnp.max(scores, axis=2, keepdims=True)
    exponent = jnp.exp(scores - top)
    total = jnp.sum(exponent, axis=2, keepdims=True)
    probs = exponent / total
    probs_low = probs.astype(low)
    mixed = jnp.einsum("hqk,kd->qhd", probs_low, value_low, preferred_element_type=jnp.float32)
    mixed_low = mixed.reshape(length, -1).astype(low)

    state_scale = lax.rsqrt(power / width_all + EPS)[:, None]
    state_low = (gated * state_scale * state_gain).astype(low)
    both_low = jnp.concatenate([mixed_low, state_low], axis=1)

    def to_slots(values):
        block = values.shape[0] // parts
        return [
            lax.dynamic_slice_in_dim(values, (place ^ mask) * block, block, 0)
            for mask in range(parts)
        ]

    mixer_shard = tensor_scatter(to_slots(product_right(both_low, out_full)))
    middle = rows_in + mixer_shard
    second, second_scale = root_norm(middle, norm_ffn_gain)
    feed_rows = jnp.concatenate(tensor_gather(second.astype(low)))
    cotangent = jnp.concatenate(cot_slots)
    grad_active = product(cotangent, down_full)
    gate_up = product(feed_rows, feed_full)
    gate_value = gate_up[:, :units]
    up_value = gate_up[:, units:]
    sigma = jax.nn.sigmoid(gate_value)
    swish = gate_value * sigma
    active = (swish * up_value).astype(low)
    grad_gate = grad_active * up_value * sigma * (1.0 + gate_value * (1.0 - sigma))
    grad_up = grad_active * swish
    grad_pair = jnp.concatenate([grad_gate, grad_up], axis=1).astype(low)
    block = length // parts

    def cut(values):
        return [values[mask * block : (mask + 1) * block] for mask in range(parts)]

    grad_second = tensor_scatter(cut(product_right(grad_pair, feed_full)))
    feed_terms = product_right(active, down_full)
    grad_second, feed_terms = lax.optimization_barrier((grad_second, feed_terms))
    feed_shard = tensor_scatter(cut(feed_terms))
    hidden_out = (middle + feed_shard).astype(low)
    grad_feed = jnp.concatenate(
        [product_left(feed_rows, grad_pair), product_left(cotangent, active)], axis=1
    ).astype(low)
    feed_sums = lax.psum_scatter(grad_feed, "dp", scatter_dimension=0, tiled=True)
    feed_sums = feed_sums.astype(jnp.float32)

    weighted_second = grad_second * norm_ffn_gain
    inner_second = jnp.sum(weighted_second * middle, axis=-1, keepdims=True)
    grad_middle = (
        out_cotangent.astype(jnp.float32)
        + second_scale * weighted_second
        - middle * second_scale**3 * inner_second / middle.shape[-1]
    )
    mixer_cot = in_order(tensor_gather(grad_middle.astype(low)), place)
    grad_both = product(mixer_cot, out_full)
    grad_out = product_left(mixer_cot, both_low).astype(low)
    grad_state = grad_both[:, 128:]
    weighted = grad_state * state_gain
    inner_sum = tensor_sum(jnp.sum(weighted * gated, axis=1))
    grad_mixed = grad_both[:, :128].astype(low).reshape(length, heads_here, HD)
    grad_probs = jnp.einsum(
        "qhd,kd->hqk", grad_mixed, value_low, preferred_element_type=jnp.float32
    )
    inner_probs = jnp.sum(probs * grad_probs, axis=2, keepdims=True)
    grad_scores = (probs * (grad_probs - inner_probs)).astype(low)
    grad_query_rot = (
        jnp.einsum("hqk,kd->qhd", grad_scores, key_low, preferred_element_type=jnp.float32) * scale
    )
    grad_query = rotate(grad_query_rot.reshape(length, -1), heads_here, -1.0)
    grad_key = rotate(
        jnp.einsum("hqk,qhd->kd", grad_scores, query_low, preferred_element_type=jnp.float32)
        * scale,
        1,
        -1.0,
    )
    grad_value = jnp.einsum(
        "hqk,qhd->kd", probs_low, grad_mixed, preferred_element_type=jnp.float32
    )
    grad_gated = state_scale * weighted - gated * state_scale**3 * inner_sum[:, None] / width_all
    grad_state_gain = jnp.sum(grad_state * gated * state_scale, axis=0)
    (
        grad_inner_raw,
        grad_write_raw,
        grad_read_raw,
        grad_step_raw,
        grad_gate_raw,
        grad_conv_weight,
        grad_conv_bias,
        grad_pair_weight,
        grad_pair_bias,
        grad_step_bias,
        grad_decay,
        grad_skip,
    ) = state_pull(grad_gated)
    grad_raw = jnp.concatenate(
        [
            grad_query,
            grad_key,
            grad_value,
            grad_write_raw,
            grad_read_raw,
            grad_gate_raw,
            grad_inner_raw,
            jnp.pad(grad_step_raw, ((0, 0), (0, 128 - heads_state))),
        ],
        axis=1,
    ).astype(low)
    grad_first = tensor_scatter(to_slots(product_right(grad_raw, mixer_full)))
    grad_mixer = product_left(mixer_rows, grad_raw).astype(low)
    out_sums = dp_scatter(grad_out)
    mixer_sums = dp_scatter(grad_mixer).astype(jnp.float32)

    grad_rows_norm, _ = root_norm_back(rows_in, first_scale, norm_in_gain, grad_first)
    gradient_hidden = grad_middle + grad_rows_norm

    rows_here = mixer_local.shape[0]
    at_rows = lax.axis_index("dp") * rows_here
    in_gain = jnp.sum(mixer_sums * mixer_local.astype(jnp.float32), axis=1, keepdims=True)
    in_gain = in_gain / lax.dynamic_slice_in_dim(norm_in_gain, at_rows, rows_here)[:, None]
    feed_local = late_local[:, 128 + width : 128 + width + 2 * units].astype(jnp.float32)
    ffn_gain = jnp.sum(feed_sums[:, : 2 * units] * feed_local, axis=1, keepdims=True)
    ffn_gain = ffn_gain / lax.dynamic_slice_in_dim(norm_ffn_gain, at_rows, rows_here)[:, None]
    shared = jnp.concatenate(
        [mixer_sums[:, 128:512], jnp.pad(jnp.concatenate([in_gain, ffn_gain], 1), ((0, 0), (0, 126)))],
        axis=1,
    ).astype(low)
    few = rows_here // parts
    terms = [
        swap(lax.dynamic_slice_in_dim(shared, (place ^ mask) * few, few, 0), "tensor", mask)
        if mask
        else lax.dynamic_slice_in_dim(shared, place * few, few, 0)
        for mask in range(parts)
    ]
    terms = [term.astype(jnp.float32) for term in terms]
    near = paired_sum(terms[: parts // 2])
    far = paired_sum(terms[parts // 2 :])
    rest = (near + far)[:, 128:]
    first_half = place < parts // 2
    heads_low = jnp.where(first_half, near[:, :128], far[:, :128])
    heads_high = jnp.where(first_half, far[:, :128], near[:, :128])
    shared = jnp.concatenate([heads_low, heads_high, rest], axis=1).astype(low)
    shared = in_order(tensor_gather(shared), place)
    shared = dp_gather(shared).astype(jnp.float32)
    gradient_key = jnp.concatenate([shared[:, :64], shared[:, 128:192]], axis=1)
    gradient_value = jnp.concatenate([shared[:, 64:128], shared[:, 192:256]], axis=1)

    small = [
        grad_pair_weight.reshape(-1),
        grad_pair_bias,
        grad_conv_weight.reshape(-1),
        grad_conv_bias,
        grad_state_gain,
        grad_step_bias,
        grad_decay,
        grad_skip,
    ]
    sizes = [item.shape[0] for item in small]
    flat = jnp.concatenate(small)
    filled = -(-flat.shape[0] // 1024) * 1024
    flat = jnp.pad(flat, (0, filled - flat.shape[0])).reshape(-1, 128)
    flat = dp_sum(flat)
    pair_rows = (sizes[0] + sizes[1]) // 128
    pair_sum = tensor_sum(flat[:pair_rows]).reshape(-1)
    flat = flat.reshape(-1)
    cuts = []
    start = 0
    for size in sizes:
        cuts.append(flat[start : start + size])
        start += size
    return (
        hidden_out,
        gradient_hidden,
        shared[:, 512],
        mixer_sums[:, :128],
        gradient_key,
        gradient_value,
        out_sums[:, :128].T.astype(jnp.float32),
        mixer_sums[:, 512 : 512 + width],
        mixer_sums[:, 512 + width : 512 + 2 * width],
        shared[:, 256:384],
        shared[:, 384:512],
        mixer_sums[:, 512 + 2 * width : 512 + 2 * width + heads_state],
        cuts[2].reshape(grad_conv_weight.shape),
        cuts[3],
        pair_sum[: sizes[0]].reshape(grad_pair_weight.shape),
        pair_sum[sizes[0] :],
        cuts[5],
        cuts[6],
        cuts[7],
        cuts[4],
        out_sums[:, 128:].T.astype(jnp.float32),
        shared[:, 513],
        feed_sums[:, :units],
        feed_sums[:, units : 2 * units],
        feed_sums[:, 2 * units :].T,
    )


def solution(mesh):
    placed = (
        P(("dp", "tensor"), None),
        P(),
        P("dp", "tensor"),
        P("dp", None),
        P("dp", None),
        P("tensor", "dp"),
        P("dp", "tensor"),
        P("dp", "tensor"),
        P("dp", None),
        P("dp", None),
        P("dp", "tensor"),
        P(None, "tensor"),
        P("tensor"),
        P(),
        P(),
        P("tensor"),
        P("tensor"),
        P("tensor"),
        P("tensor"),
        P("tensor", "dp"),
        P(),
        P("dp", "tensor"),
        P("dp", "tensor"),
        P("tensor", "dp"),
        P(("dp", "tensor"), None),
    )
    return jax.shard_map(
        body,
        mesh=mesh,
        in_specs=placed,
        out_specs=(
            P(("dp", "tensor"), None),
            P(("dp", "tensor"), None),
            P(),
            P("dp", "tensor"),
            P(),
            P(),
            P("tensor", "dp"),
            P("dp", "tensor"),
            P("dp", "tensor"),
            P(),
            P(),
            P("dp", "tensor"),
            P(None, "tensor"),
            P("tensor"),
            P(),
            P(),
            P("tensor"),
            P("tensor"),
            P("tensor"),
            P("tensor"),
            P("tensor", "dp"),
            P(),
            P("dp", "tensor"),
            P("dp", "tensor"),
            P("tensor", "dp"),
        ),
        check_vma=False,
    )
```

time: 1060 us -> 577 us (0.54)
  waiting for transfers between devices: 560 us -> 118 us
  blocking collectives: 163 us -> 0 us
  starting transfers between devices: 1.3 us -> 117 us
  matrix products: 126 us -> 77.3 us
  local copies, waits for them, and re-layouts: 130 us -> 164 us
  other arithmetic: 55 us -> 73.5 us
    reduce_scatter x13 -> x0, waiting for transfers between devices: 437 us -> none  [the longest x1 45.2 us: body(): lax.psum_scatter(grad_feed_down, 'dp', scatter_dimension=1, tiled=True)]
    all_gather x7 -> x1, waiting for transfers between devices: 120 us -> 0.02 us  [body(): late_full = lax.all_gather(late_local, 'dp', axis=0, tiled=True)]
    ppermute x0 -> x61, waiting for transfers between devices: none -> 118 us  [swap(): lax.ppermute(values, axis, [(index, index ^ mask) for index in range(size)])]
    ppermute x0 -> x61, starting transfers between devices: none -> 117 us  [swap(): lax.ppermute(values, axis, [(index, index ^ mask) for index in range(size)])]
    all_gather x10 -> x0, blocking collectives: 99.7 us -> none  [the longest x1 11.2 us: body(): lax.all_gather(gate_weight, 'dp', axis=0, tiled=True)]
    psum x3 -> x0, blocking collectives: 63.4 us -> none  [the longest x1 41.3 us: body(): lax.psum((grad_in_gain, grad_ffn_gain, key_spread, value_spread, grad_wri...]
    dot_general x13 -> x4, matrix products: 22.3 us -> 6.31 us  [product(): return jnp.dot(left, right, preferred_element_type=jnp.float32)]
    dot_general x11 -> x4, matrix products: 21.7 us -> 7.35 us  [product_left(): lax.dot_general(left, right, (((0,), (0,)), ((), ())), preferred_element_...]
  transfers between devices with their start and end apart: 21 -> 63, of which waited for: 17 -> 24; matrix products, arithmetic and copies ran while one was open for 6% -> 50% of each run, Pallas kernels for 0% -> 0%
where the time goes in v1:
time: 577 us; the launch traced here: 567 us
  local copies, waits for them, and re-layouts  164 us (28%)
  waiting for transfers between devices  118 us (20%)
  starting transfers between devices  117 us (20%)
  matrix products  77.3 us (13%)
  other arithmetic  73.5 us (13%)
  between operations  16.2 us (3%)
    ppermute x61, waiting for transfers between devices, swap(): lax.ppermute(values, axis, [(index, index ^ mask) for index in range(size)])  118 us
    ppermute x61, starting transfers between devices, swap(): lax.ppermute(values, axis, [(index, index ^ mask) for index in range(size)])  117 us
    dynamic_update_slice x12, local copies, waits for them, and re-layouts, mixer_state(): final, outputs = lax.scan(jax.checkpoint(state_block), start, blocks)  42.2 us
    unnamed x205, local copies, waits for them, and re-layouts  29.5 us
    squeeze x20, local copies, waits for them, and re-layouts, mixer_state(): final, outputs = lax.scan(jax.checkpoint(state_block), start, blocks)  17.9 us
    dot_general x12, matrix products, state_block(): jnp.einsum('tsh,shp->thp', intersection[:, :, None] * weights, scaled, pr...  16.4 us
  transfers between devices with their start and end apart: 63, of which 24 were waited for; matrix products, arithmetic and copies ran while one was open for 50% of the time, Pallas kernels for 0%

profile of v1, /device:TPU:0, one launch (start us, length us, event | category | flops | bytes accessed | tf_op | source)
XLA Modules:
  0.0 566.9 jit_solution(18335902163855239650)
XLA Ops:
  10.7 2.6 collective-permute-start.4
  24.1 2.7 collective-permute-start.1
  26.8 4.6 collective-permute-done.6
  31.4 3.6 collective-permute-start.2
  37.9 7.1 %collective-permute-done.1 = bf16[128,1024]{1,0:T(8,128)(2,1)S(1)} collective-permute-done((bf16[128,1024]{1,0:T(8,128)(2,1)}, bf16[128,1024]{1,0:T(8,128)(2,1)S(1)}, u32[]{:S(2)}, u32[]{:S(2)}) %collective-permute-start.1) | collective-permute-done | bytes 262176 | tf_op jit(solution)/shard_map/ppermute | solution.py:138
  52.0 2.5 copy.271
  58.0 2.4 copy.275
  69.0 57.6 %while.39 = (s32[]{:T(128)}, f32[6,64,128]{2,1,0:T(8,128)S(1)}, f32[4,128,6,64]{1,0,3,2:T(4,128)}, f32[4,6,64,128]{3,2,1,0:T(8,128)}, f32[4,128,6]{2,1,0:T(8,128...) while((s32[]{:T(128)}, f32[6,64,128]{2,1,0:T(8,128)S(1)}, ...), condition=%wide.region_5.6_spmd.clone, body=%wide.region_3.5_spmd.clone.sunk | while | flops 252444672 | bytes 2827037 | solution.py:131
  71.3 2.5 convolution_bitcast_fusion.10
  75.2 6.0 %dynamic_update_slice.147 = f32[4,128,6,64]{1,0,3,2:T(4,128)} dynamic-update-slice(f32[4,128,6,64]{1,0,3,2:T(4,128)} %get-tuple-element.1042, f32[1,128,6,64]{1,0,3,2:T(1,128)S(1)} %bitcast.464, s32[]{:T(128)} %get-tuple-element.1040, s32[]{:T(128)} %constant.258.clone.1..sunk, s32[]{:T(128)} %constant.258.clone.1..sunk, s32[]{:T(128)} %constant.258.clone.1..sunk) | dynamic-update-slice | bytes 393220 | tf_op jit(solution)/shard_map/jvp()/while/body/jit(dynamic_update_index_in_dim)/dynamic_update_slice | solution.py:131
  85.6 2.5 convolution_bitcast_fusion.10
  89.5 6.0 %dynamic_update_slice.147 = f32[4,128,6,64]{1,0,3,2:T(4,128)} dynamic-update-slice(f32[4,128,6,64]{1,0,3,2:T(4,128)} %get-tuple-element.1042, f32[1,128,6,64]{1,0,3,2:T(1,128)S(1)} %bitcast.464, s32[]{:T(128)} %get-tuple-element.1040, s32[]{:T(128)} %constant.258.clone.1..sunk, s32[]{:T(128)} %constant.258.clone.1..sunk, s32[]{:T(128)} %constant.258.clone.1..sunk) | dynamic-update-slice | bytes 393220 | tf_op jit(solution)/shard_map/jvp()/while/body/jit(dynamic_update_index_in_dim)/dynamic_update_slice | solution.py:131
  99.9 2.5 convolution_bitcast_fusion.10
  103.8 6.0 %dynamic_update_slice.147 = f32[4,128,6,64]{1,0,3,2:T(4,128)} dynamic-update-slice(f32[4,128,6,64]{1,0,3,2:T(4,128)} %get-tuple-element.1042, f32[1,128,6,64]{1,0,3,2:T(1,128)S(1)} %bitcast.464, s32[]{:T(128)} %get-tuple-element.1040, s32[]{:T(128)} %constant.258.clone.1..sunk, s32[]{:T(128)} %constant.258.clone.1..sunk, s32[]{:T(128)} %constant.258.clone.1..sunk) | dynamic-update-slice | bytes 393220 | tf_op jit(solution)/shard_map/jvp()/while/body/jit(dynamic_update_index_in_dim)/dynamic_update_slice | solution.py:131
  114.1 2.5 convolution_bitcast_fusion.10
  118.1 6.0 %dynamic_update_slice.147 = f32[4,128,6,64]{1,0,3,2:T(4,128)} dynamic-update-slice(f32[4,128,6,64]{1,0,3,2:T(4,128)} %get-tuple-element.1042, f32[1,128,6,64]{1,0,3,2:T(1,128)S(1)} %bitcast.464, s32[]{:T(128)} %get-tuple-element.1040, s32[]{:T(128)} %constant.258.clone.1..sunk, s32[]{:T(128)} %constant.258.clone.1..sunk, s32[]{:T(128)} %constant.258.clone.1..sunk) | dynamic-update-slice | bytes 393220 | tf_op jit(solution)/shard_map/jvp()/while/body/jit(dynamic_update_index_in_dim)/dynamic_update_slice | solution.py:131
  128.7 2.3 copy.279
  131.1 2.7 multiply_reduce_fusion.12
  133.8 2.7 collective-permute-start.10
  136.4 4.0 collective-permute-start.8
  142.8 3.3 fusion.183
  165.4 2.3 copy.296
  168.7 2.7 collective-permute-done.11
  171.4 2.5 collective-permute-start.16
  173.9 5.7 %collective-permute-done.12 = bf16[128,1024]{1,0:T(8,128)(2,1)} collective-permute-done((bf16[128,1024]{1,0:T(8,128)(2,1)}, bf16[128,1024]{1,0:T(8,128)(2,1)}, u32[]{:S(2)}, u32[]{:S(2)}) %collective-permute-start.12) | collective-permute-done | bytes 262176 | tf_op jit(solution)/shard_map/ppermute | solution.py:138
  181.3 22.8 %collective-permute-start.17 = (bf16[128,1024]{1,0:T(8,128)(2,1)S(1)}, bf16[128,1024]{1,0:T(8,128)(2,1)S(1)}, u32[]{:S(2)}, u32[]{:S(2)}) collective-permute-start(bf16[128,1024]{1,0:T(8,128)(2,1)S(1)} %multiply_convert_fusion.4), channel_id=1, source_target_pairs={{0,1},{1,0},{2,3},{3,2},{4,5},{5,4},{6,7},{7,6},{8,9},{9,8},{10,11... | collective-permute-start | bytes 786440 | tf_op jit(solution)/shard_map/ppermute | solution.py:138
  208.5 2.3 collective-permute-done.17
  210.9 13.3 %collective-permute-done.18 = bf16[128,1024]{1,0:T(8,128)(2,1)S(1)} collective-permute-done((bf16[128,1024]{1,0:T(8,128)(2,1)S(1)}, bf16[128,1024]{1,0:T(8,128)(2,1)S(1)}, u32[]{:S(2)}, u32[]{:S(2)}) %collective-permute-start.18) | collective-permute-done | bytes 262176 | tf_op jit(solution)/shard_map/ppermute | solution.py:138
  227.9 3.5 collective-permute-start.20
  235.4 3.5 collective-permute-done.20
  238.8 13.0 %collective-permute-done.21 = bf16[128,1024]{1,0:T(8,128)(2,1)S(1)} collective-permute-done((bf16[128,1024]{1,0:T(8,128)(2,1)S(1)}, bf16[128,1024]{1,0:T(8,128)(2,1)S(1)}, u32[]{:S(2)}, u32[]{:S(2)}) %collective-permute-start.21) | collective-permute-done | bytes 262176 | tf_op jit(solution)/shard_map/ppermute | solution.py:138
  252.2 3.4 collective-permute-start.23
  259.7 3.2 collective-permute-done.23
  262.9 13.0 %collective-permute-done.24 = bf16[128,1024]{1,0:T(8,128)(2,1)S(1)} collective-permute-done((bf16[128,1024]{1,0:T(8,128)(2,1)S(1)}, bf16[128,1024]{1,0:T(8,128)(2,1)S(1)}, u32[]{:S(2)}, u32[]{:S(2)}) %collective-permute-start.24) | collective-permute-done | bytes 262176 | tf_op jit(solution)/shard_map/ppermute | solution.py:138
  277.3 3.4 collective-permute-start.26
  286.1 4.7 copy.326
  290.9 11.5 %collective-permute-done.27 = bf16[128,1024]{1,0:T(8,128)(2,1)} collective-permute-done((bf16[128,1024]{1,0:T(8,128)(2,1)}, bf16[128,1024]{1,0:T(8,128)(2,1)}, u32[]{:S(2)}, u32[]{:S(2)}) %collective-permute-start.27) | collective-permute-done | bytes 262176 | tf_op jit(solution)/shard_map/ppermute | solution.py:138
  306.9 3.4 collective-permute-start.29
  317.8 2.9 fusion.75
  338.8 4.2 multiply_reduce_fusion.4
  347.2 67.6 %while.40 = (s32[]{:T(128)}, f32[6,64,128]{2,1,0:T(8,128)S(1)}, f32[4,128,6,64]{1,0,3,2:T(4,128)S(1)}, f32[4,128,6]{2,1,0:T(8,128)}, f32[4,128,128]{2,1,0:T(8,12...) while((s32[]{:T(128)}, f32[6,64,128]{2,1,0:T(8,128)S(1)}, ...), condition=%wide.region_20.21_spmd.clone, body=%wide.region_11.20_spmd.clone.sunk | while | flops 606080768 | bytes 7453199 | solution.py:131
  358.1 4.0 dynamic_update_slice.151
  375.0 4.0 dynamic_update_slice.151
  391.8 4.0 dynamic_update_slice.151
  408.7 4.0 dynamic_update_slice.151
  416.3 2.5 reshape.540
  423.2 4.8 multiply_reduce_fusion.8
  428.6 3.6 multiply_reduce_fusion.16
  433.9 2.4 fusion.166
  443.5 2.9 concatenate.109
  446.4 3.7 convolution_convert_fusion
  459.2 2.5 collective-permute-done.57
  463.7 2.4 collective-permute-start.59
  469.3 3.0 collective-permute-start.33
  475.5 5.0 collective-permute-done.32
  480.5 10.2 %collective-permute-done.33 = bf16[128,1024]{1,0:T(8,128)(2,1)} collective-permute-done((bf16[128,1024]{1,0:T(8,128)(2,1)}, bf16[128,1024]{1,0:T(8,128)(2,1)}, u32[]{:S(2)}, u32[]{:S(2)}) %collective-permute-start.33) | collective-permute-done | bytes 262176 | tf_op jit(solution)/shard_map/ppermute | solution.py:138
  494.7 2.4 collective-permute-start.53
  500.1 2.4 collective-permute-start.38
  502.5 2.3 fusion.105
  505.0 4.0 collective-permute-done.36
  509.0 4.1 collective-permute-done.37
  516.0 6.4 %collective-permute-start.39 = (bf16[32,512]{1,0:T(8,128)(2,1)S(1)}, bf16[32,512]{1,0:T(8,128)(2,1)S(1)}, u32[]{:S(2)}, u32[]{:S(2)}) collective-permute-start(bf16[32,512]{1,0:T(8,128)(2,1)S(1)} %get-tuple-element.830), channel_id=1, source_target_pairs={{0,1},{1,0},{2,3},{3,2},{4,5},{5,4},{6,7},{7,6},{8,9},{9,8},{10,11... | collective-permute-start | bytes 98312 | tf_op jit(solution)/shard_map/ppermute | solution.py:138
  525.5 2.4 collective-permute-done.40
  543.4 3.5 collective-permute-done.47
  (657 shorter events, 267.4 us)
Async XLA Ops:
  7.3 143.8 %all-gather.2.cloned.1.call-start = ((), (), s32[]{:S(2)}) async-start(), calls=%async_computation.1 | async-start | bytes 4718592 | tf_op jit(solution)/shard_map/all_gather | solution.py:277
  10.2 36.3 %collective-permute-start.3 = (bf16[128,1408]{1,0:T(8,128)(2,1)S(1)}, bf16[128,1408]{1,0:T(8,128)(2,1)}, u32[]{:S(2)}, u32[]{:S(2)}) collective-permute-start(bf16[128,1408]{1,0:T(8,128)(2,1)S(1)} %concatenate.97), channel_id=1, source_target_pairs={{0,4},{4,0},{8,12},{12,8},{16,20},{20,16},{24,28},{28,24},{1,5},{5... | collective-permute-start | bytes 1081352 | tf_op jit(solution)/shard_map/ppermute | solution.py:138
  10.7 13.4 %collective-permute-start.4 = (bf16[128,1408]{1,0:T(8,128)(2,1)S(1)}, bf16[128,1408]{1,0:T(8,128)(2,1)S(1)}, u32[]{:S(2)}, u32[]{:S(2)}) collective-permute-start(bf16[128,1408]{1,0:T(8,128)(2,1)S(1)} %concatenate.97), channel_id=1, source_target_pairs={{0,8},{4,12},{8,0},{12,4},{16,24},{20,28},{24,16},{28,20},{1,9},{5... | collective-permute-start | bytes 1081352 | tf_op jit(solution)/shard_map/ppermute | solution.py:138
  13.3 18.1 %collective-permute-start.6 = (bf16[128,1408]{1,0:T(8,128)(2,1)S(1)}, bf16[128,1408]{1,0:T(8,128)(2,1)S(1)}, u32[]{:S(2)}, u32[]{:S(2)}) collective-permute-start(bf16[128,1408]{1,0:T(8,128)(2,1)S(1)} %concatenate.97), channel_id=1, source_target_pairs={{0,24},{4,28},{8,16},{12,20},{16,8},{20,12},{24,0},{28,4},{1,25},{... | collective-permute-start | bytes 1081352 | tf_op jit(solution)/shard_map/ppermute | solution.py:138
  14.8 20.2 %collective-permute-start.5 = (bf16[128,1408]{1,0:T(8,128)(2,1)S(1)}, bf16[128,1408]{1,0:T(8,128)(2,1)S(1)}, u32[]{:S(2)}, u32[]{:S(2)}) collective-permute-start(bf16[128,1408]{1,0:T(8,128)(2,1)S(1)} %concatenate.97), channel_id=1, source_target_pairs={{0,16},{4,20},{8,24},{12,28},{16,0},{20,4},{24,8},{28,12},{1,17},{... | collective-permute-start | bytes 1081352 | tf_op jit(solution)/shard_map/ppermute | solution.py:138
  18.3 19.6 %collective-permute-start = (bf16[128,1024]{1,0:T(8,128)(2,1)}, bf16[128,1024]{1,0:T(8,128)(2,1)}, u32[]{:S(2)}, u32[]{:S(2)}) collective-permute-start(bf16[128,1024]{1,0:T(8,128)(2,1)} %fusion.101), channel_id=1, source_target_pairs={{0,1},{1,0},{2,3},{3,2},{4,5},{5,4},{6,7},{7,6},{8,9},{9,8},{10,11... | collective-permute-start | bytes 786440 | tf_op jit(solution)/shard_map/ppermute | solution.py:138
  22.5 491.1 %reduce-scatter.4.cloned.1.call-start = ((), (), s32[]{:S(2)}) async-start(), calls=%async_computation.2 | async-start | bytes 3538944
  24.1 20.9 %collective-permute-start.1 = (bf16[128,1024]{1,0:T(8,128)(2,1)}, bf16[128,1024]{1,0:T(8,128)(2,1)S(1)}, u32[]{:S(2)}, u32[]{:S(2)}) collective-permute-start(bf16[128,1024]{1,0:T(8,128)(2,1)} %fusion.101), channel_id=1, source_target_pairs={{0,2},{1,3},{2,0},{3,1},{4,6},{5,7},{6,4},{7,5},{8,10},{9,11},{10,... | collective-permute-start | bytes 786440 | tf_op jit(solution)/shard_map/ppermute | solution.py:138
  31.4 13.7 %collective-permute-start.2 = (bf16[128,1024]{1,0:T(8,128)(2,1)}, bf16[128,1024]{1,0:T(8,128)(2,1)}, u32[]{:S(2)}, u32[]{:S(2)}) collective-permute-start(bf16[128,1024]{1,0:T(8,128)(2,1)} %fusion.101), channel_id=1, source_target_pairs={{0,3},{1,2},{2,1},{3,0},{4,7},{5,6},{6,5},{7,4},{8,11},{9,10},{10,... | collective-permute-start | bytes 786440 | tf_op jit(solution)/shard_map/ppermute | solution.py:138
  36.2 12.1 %collective-permute-start.7 = (bf16[3,128,1408]{2,1,0:T(8,128)(2,1)}, bf16[3,128,1408]{2,1,0:T(8,128)(2,1)S(1)}, u32[]{:S(2)}, u32[]{:S(2)}) collective-permute-start(bf16[3,128,1408]{2,1,0:T(8,128)(2,1)} %pad_maximum_fusion.1), channel_id=1, source_target_pairs={{0,4},{4,0},{8,12},{12,8},{16,20},{20,16},{24,28},{28,24},{1,5},{5... | collective-permute-start | bytes 3244040 | tf_op jit(solution)/shard_map/ppermute | solution.py:138
  52.0 286.8 %copy-start = (f32[512,1408]{1,0:T(8,128)}, f32[512,1408]{1,0:T(8,128)S(1)}, u32[]{:S(2)}) copy-start(f32[512,1408]{1,0:T(8,128)S(1)} %fusion.130) | copy-start | bytes 8650756
  133.8 14.7 %collective-permute-start.10 = (f32[512]{0:T(512)S(1)}, f32[512]{0:T(512)}, u32[]{:S(2)}, u32[]{:S(2)}) collective-permute-start(f32[512]{0:T(512)S(1)} %get-tuple-element.744), channel_id=1, source_target_pairs={{0,3},{1,2},{2,1},{3,0},{4,7},{5,6},{6,5},{7,4},{8,11},{9,10},{10,... | collective-permute-start | bytes 6152 | tf_op jit(solution)/shard_map/ppermute | solution.py:138
  136.4 12.0 %collective-permute-start.8 = (f32[512]{0:T(512)S(1)}, f32[512]{0:T(512)}, u32[]{:S(2)}, u32[]{:S(2)}) collective-permute-start(f32[512]{0:T(512)S(1)} %get-tuple-element.744), channel_id=1, source_target_pairs={{0,1},{1,0},{2,3},{3,2},{4,5},{5,4},{6,7},{7,6},{8,9},{9,8},{10,11... | collective-permute-start | bytes 6152 | tf_op jit(solution)/shard_map/ppermute | solution.py:138
  140.4 8.0 %collective-permute-start.9 = (f32[512]{0:T(512)S(1)}, f32[512]{0:T(512)}, u32[]{:S(2)}, u32[]{:S(2)}) collective-permute-start(f32[512]{0:T(512)S(1)} %get-tuple-element.744), channel_id=1, source_target_pairs={{0,2},{1,3},{2,0},{3,1},{4,6},{5,7},{6,4},{7,5},{8,10},{9,11},{10,... | collective-permute-start | bytes 6152 | tf_op jit(solution)/shard_map/ppermute | solution.py:138
  156.0 15.4 %collective-permute-start.11 = (bf16[128,1024]{1,0:T(8,128)(2,1)}, bf16[128,1024]{1,0:T(8,128)(2,1)}, u32[]{:S(2)}, u32[]{:S(2)}) collective-permute-start(bf16[128,1024]{1,0:T(8,128)(2,1)} %get-tuple-element.770), channel_id=1, source_target_pairs={{0,1},{1,0},{2,3},{3,2},{4,5},{5,4},{6,7},{7,6},{8,9},{9,8},{10,11... | collective-permute-start | bytes 786440 | tf_op jit(solution)/shard_map/ppermute | solution.py:138
  157.9 21.8 %collective-permute-start.12 = (bf16[128,1024]{1,0:T(8,128)(2,1)}, bf16[128,1024]{1,0:T(8,128)(2,1)}, u32[]{:S(2)}, u32[]{:S(2)}) collective-permute-start(bf16[128,1024]{1,0:T(8,128)(2,1)} %get-tuple-element.772), channel_id=1, source_target_pairs={{0,2},{1,3},{2,0},{3,1},{4,6},{5,7},{6,4},{7,5},{8,10},{9,11},{10,... | collective-permute-start | bytes 786440 | tf_op jit(solution)/shard_map/ppermute | solution.py:138
  159.0 20.7 %collective-permute-start.13 = (bf16[128,1024]{1,0:T(8,128)(2,1)}, bf16[128,1024]{1,0:T(8,128)(2,1)}, u32[]{:S(2)}, u32[]{:S(2)}) collective-permute-start(bf16[128,1024]{1,0:T(8,128)(2,1)} %get-tuple-element.771), channel_id=1, source_target_pairs={{0,3},{1,2},{2,1},{3,0},{4,7},{5,6},{6,5},{7,4},{8,11},{9,10},{10,... | collective-permute-start | bytes 786440 | tf_op jit(solution)/shard_map/ppermute | solution.py:138
  160.4 44.4 %collective-permute-start.14 = (bf16[128,1024]{1,0:T(8,128)(2,1)}, bf16[128,1024]{1,0:T(8,128)(2,1)}, u32[]{:S(2)}, u32[]{:S(2)}) collective-permute-start(bf16[128,1024]{1,0:T(8,128)(2,1)} %param.53), channel_id=1, source_target_pairs={{0,1},{1,0},{2,3},{3,2},{4,5},{5,4},{6,7},{7,6},{8,9},{9,8},{10,11... | collective-permute-start | bytes 786440 | tf_op jit(solution)/shard_map/ppermute | solution.py:138
  161.4 46.1 %collective-permute-start.15 = (bf16[128,1024]{1,0:T(8,128)(2,1)}, bf16[128,1024]{1,0:T(8,128)(2,1)}, u32[]{:S(2)}, u32[]{:S(2)}) collective-permute-start(bf16[128,1024]{1,0:T(8,128)(2,1)} %param.53), channel_id=1, source_target_pairs={{0,2},{1,3},{2,0},{3,1},{4,6},{5,7},{6,4},{7,5},{8,10},{9,11},{10,... | collective-permute-start | bytes 786440 | tf_op jit(solution)/shard_map/ppermute | solution.py:138
  171.4 37.1 %collective-permute-start.16 = (bf16[128,1024]{1,0:T(8,128)(2,1)}, bf16[128,1024]{1,0:T(8,128)(2,1)S(1)}, u32[]{:S(2)}, u32[]{:S(2)}) collective-permute-start(bf16[128,1024]{1,0:T(8,128)(2,1)} %param.53), channel_id=1, source_target_pairs={{0,3},{1,2},{2,1},{3,0},{4,7},{5,6},{6,5},{7,4},{8,11},{9,10},{10,... | collective-permute-start | bytes 786440 | tf_op jit(solution)/shard_map/ppermute | solution.py:138
  181.3 29.5 %collective-permute-start.17 = (bf16[128,1024]{1,0:T(8,128)(2,1)S(1)}, bf16[128,1024]{1,0:T(8,128)(2,1)S(1)}, u32[]{:S(2)}, u32[]{:S(2)}) collective-permute-start(bf16[128,1024]{1,0:T(8,128)(2,1)S(1)} %multiply_convert_fusion.4), channel_id=1, source_target_pairs={{0,1},{1,0},{2,3},{3,2},{4,5},{5,4},{6,7},{7,6},{8,9},{9,8},{10,11... | collective-permute-start | bytes 786440 | tf_op jit(solution)/shard_map/ppermute | solution.py:138
  204.1 20.1 %collective-permute-start.18 = (bf16[128,1024]{1,0:T(8,128)(2,1)S(1)}, bf16[128,1024]{1,0:T(8,128)(2,1)S(1)}, u32[]{:S(2)}, u32[]{:S(2)}) collective-permute-start(bf16[128,1024]{1,0:T(8,128)(2,1)S(1)} %multiply_convert_fusion.4), channel_id=1, source_target_pairs={{0,2},{1,3},{2,0},{3,1},{4,6},{5,7},{6,4},{7,5},{8,10},{9,11},{10,... | collective-permute-start | bytes 786440 | tf_op jit(solution)/shard_map/ppermute | solution.py:138
  204.8 19.4 %collective-permute-start.19 = (bf16[128,1024]{1,0:T(8,128)(2,1)S(1)}, bf16[128,1024]{1,0:T(8,128)(2,1)S(1)}, u32[]{:S(2)}, u32[]{:S(2)}) collective-permute-start(bf16[128,1024]{1,0:T(8,128)(2,1)S(1)} %multiply_convert_fusion.4), channel_id=1, source_target_pairs={{0,3},{1,2},{2,1},{3,0},{4,7},{5,6},{6,5},{7,4},{8,11},{9,10},{10,... | collective-permute-start | bytes 786440 | tf_op jit(solution)/shard_map/ppermute | solution.py:138
  227.9 10.9 %collective-permute-start.20 = (bf16[128,1024]{1,0:T(8,128)(2,1)S(1)}, bf16[128,1024]{1,0:T(8,128)(2,1)S(1)}, u32[]{:S(2)}, u32[]{:S(2)}) collective-permute-start(bf16[128,1024]{1,0:T(8,128)(2,1)S(1)} %get-tuple-element.791), channel_id=1, source_target_pairs={{0,1},{1,0},{2,3},{3,2},{4,5},{5,4},{6,7},{7,6},{8,9},{9,8},{10,11... | collective-permute-start | bytes 786440 | tf_op jit(solution)/shard_map/ppermute | solution.py:138
  231.5 20.3 %collective-permute-start.21 = (bf16[128,1024]{1,0:T(8,128)(2,1)S(1)}, bf16[128,1024]{1,0:T(8,128)(2,1)S(1)}, u32[]{:S(2)}, u32[]{:S(2)}) collective-permute-start(bf16[128,1024]{1,0:T(8,128)(2,1)S(1)} %get-tuple-element.793), channel_id=1, source_target_pairs={{0,2},{1,3},{2,0},{3,1},{4,6},{5,7},{6,4},{7,5},{8,10},{9,11},{10,... | collective-permute-start | bytes 786440 | tf_op jit(solution)/shard_map/ppermute | solution.py:138
  232.5 19.3 %collective-permute-start.22 = (bf16[128,1024]{1,0:T(8,128)(2,1)S(1)}, bf16[128,1024]{1,0:T(8,128)(2,1)S(1)}, u32[]{:S(2)}, u32[]{:S(2)}) collective-permute-start(bf16[128,1024]{1,0:T(8,128)(2,1)S(1)} %get-tuple-element.792), channel_id=1, source_target_pairs={{0,3},{1,2},{2,1},{3,0},{4,7},{5,6},{6,5},{7,4},{8,11},{9,10},{10,... | collective-permute-start | bytes 786440 | tf_op jit(solution)/shard_map/ppermute | solution.py:138
  252.2 10.7 %collective-permute-start.23 = (bf16[128,1024]{1,0:T(8,128)(2,1)S(1)}, bf16[128,1024]{1,0:T(8,128)(2,1)S(1)}, u32[]{:S(2)}, u32[]{:S(2)}) collective-permute-start(bf16[128,1024]{1,0:T(8,128)(2,1)S(1)} %get-tuple-element.788), channel_id=1, source_target_pairs={{0,1},{1,0},{2,3},{3,2},{4,5},{5,4},{6,7},{7,6},{8,9},{9,8},{10,11... | collective-permute-start | bytes 786440 | tf_op jit(solution)/shard_map/ppermute | solution.py:138
  255.6 20.3 %collective-permute-start.24 = (bf16[128,1024]{1,0:T(8,128)(2,1)S(1)}, bf16[128,1024]{1,0:T(8,128)(2,1)S(1)}, u32[]{:S(2)}, u32[]{:S(2)}) collective-permute-start(bf16[128,1024]{1,0:T(8,128)(2,1)S(1)} %get-tuple-element.790), channel_id=1, source_target_pairs={{0,2},{1,3},{2,0},{3,1},{4,6},{5,7},{6,4},{7,5},{8,10},{9,11},{10,... | collective-permute-start | bytes 786440 | tf_op jit(solution)/shard_map/ppermute | solution.py:138
  256.9 19.0 %collective-permute-start.25 = (bf16[128,1024]{1,0:T(8,128)(2,1)S(1)}, bf16[128,1024]{1,0:T(8,128)(2,1)S(1)}, u32[]{:S(2)}, u32[]{:S(2)}) collective-permute-start(bf16[128,1024]{1,0:T(8,128)(2,1)S(1)} %get-tuple-element.789), channel_id=1, source_target_pairs={{0,3},{1,2},{2,1},{3,0},{4,7},{5,6},{6,5},{7,4},{8,11},{9,10},{10,... | collective-permute-start | bytes 786440 | tf_op jit(solution)/shard_map/ppermute | solution.py:138
  277.3 13.5 %collective-permute-start.26 = (bf16[128,1024]{1,0:T(8,128)(2,1)}, bf16[128,1024]{1,0:T(8,128)(2,1)}, u32[]{:S(2)}, u32[]{:S(2)}) collective-permute-start(bf16[128,1024]{1,0:T(8,128)(2,1)} %get-tuple-element.740), channel_id=1, source_target_pairs={{0,1},{1,0},{2,3},{3,2},{4,5},{5,4},{6,7},{7,6},{8,9},{9,8},{10,11... | collective-permute-start | bytes 786440 | tf_op jit(solution)/shard_map/ppermute | solution.py:138
  280.7 21.7 %collective-permute-start.27 = (bf16[128,1024]{1,0:T(8,128)(2,1)}, bf16[128,1024]{1,0:T(8,128)(2,1)}, u32[]{:S(2)}, u32[]{:S(2)}) collective-permute-start(bf16[128,1024]{1,0:T(8,128)(2,1)} %get-tuple-element.740), channel_id=1, source_target_pairs={{0,2},{1,3},{2,0},{3,1},{4,6},{5,7},{6,4},{7,5},{8,10},{9,11},{10,... | collective-permute-start | bytes 786440 | tf_op jit(solution)/shard_map/ppermute | solution.py:138
  282.6 19.8 %collective-permute-start.28 = (bf16[128,1024]{1,0:T(8,128)(2,1)}, bf16[128,1024]{1,0:T(8,128)(2,1)}, u32[]{:S(2)}, u32[]{:S(2)}) collective-permute-start(bf16[128,1024]{1,0:T(8,128)(2,1)} %get-tuple-element.740), channel_id=1, source_target_pairs={{0,3},{1,2},{2,1},{3,0},{4,7},{5,6},{6,5},{7,4},{8,11},{9,10},{10,... | collective-permute-start | bytes 786440 | tf_op jit(solution)/shard_map/ppermute | solution.py:138
  306.9 31.2 %collective-permute-start.29 = (f32[512]{0:T(512)S(1)}, f32[512]{0:T(512)}, u32[]{:S(2)}, u32[]{:S(2)}) collective-permute-start(f32[512]{0:T(512)S(1)} %get-tuple-element.671), channel_id=1, source_target_pairs={{0,1},{1,0},{2,3},{3,2},{4,5},{5,4},{6,7},{7,6},{8,9},{9,8},{10,11... | collective-permute-start | bytes 6152 | tf_op jit(solution)/shard_map/ppermute | solution.py:138
  310.4 27.8 %collective-permute-start.30 = (f32[512]{0:T(512)S(1)}, f32[512]{0:T(512)}, u32[]{:S(2)}, u32[]{:S(2)}) collective-permute-start(f32[512]{0:T(512)S(1)} %get-tuple-element.671), channel_id=1, source_target_pairs={{0,2},{1,3},{2,0},{3,1},{4,6},{5,7},{6,4},{7,5},{8,10},{9,11},{10,... | collective-permute-start | bytes 6152 | tf_op jit(solution)/shard_map/ppermute | solution.py:138
  312.2 25.9 %collective-permute-start.31 = (f32[512]{0:T(512)S(1)}, f32[512]{0:T(512)}, u32[]{:S(2)}, u32[]{:S(2)}) collective-permute-start(f32[512]{0:T(512)S(1)} %get-tuple-element.671), channel_id=1, source_target_pairs={{0,3},{1,2},{2,1},{3,0},{4,7},{5,6},{6,5},{7,4},{8,11},{9,10},{10,... | collective-permute-start | bytes 6152 | tf_op jit(solution)/shard_map/ppermute | solution.py:138
  329.1 163.1 %collective-permute-start.50 = (bf16[4,128,512]{1,2,0:T(8,128)(2,1)}, bf16[4,128,512]{1,2,0:T(8,128)(2,1)}, u32[]{:S(2)}, u32[]{:S(2)}) collective-permute-start(bf16[4,128,512]{1,2,0:T(8,128)(2,1)} %bitcast.485), channel_id=1, source_target_pairs={{0,4},{4,0},{8,12},{12,8},{16,20},{20,16},{24,28},{28,24},{1,5},{5... | collective-permute-start | bytes 1572872 | tf_op jit(solution)/shard_map/ppermute | solution.py:138
  439.2 14.1 %collective-permute-start.54 = (f32[32,128]{1,0:T(8,128)}, f32[32,128]{1,0:T(8,128)}, u32[]{:S(2)}, u32[]{:S(2)}) collective-permute-start(f32[32,128]{1,0:T(8,128)} %pad_bitcast_fusion), channel_id=1, source_target_pairs={{0,4},{4,0},{8,12},{12,8},{16,20},{20,16},{24,28},{28,24},{1,5},{5... | collective-permute-start | bytes 49160 | tf_op jit(solution)/shard_map/ppermute | solution.py:138
  453.3 43.8 %collective-permute-start.35 = (bf16[4,128,1408]{2,1,0:T(8,128)(2,1)}, bf16[4,128,1408]{2,1,0:T(8,128)(2,1)}, u32[]{:S(2)}, u32[]{:S(2)}) collective-permute-start(bf16[4,128,1408]{2,1,0:T(8,128)(2,1)} %dynamic-slice_bitcast_fusion.6), channel_id=1, source_target_pairs={{0,4},{4,0},{8,12},{12,8},{16,20},{20,16},{24,28},{28,24},{1,5},{5... | collective-permute-start | bytes 4325384 | tf_op jit(solution)/shard_map/ppermute | solution.py:138
  454.0 4.4 collective-permute-start.55
  455.5 3.7 collective-permute-start.56
  457.1 4.6 collective-permute-start.57
  463.1 6.2 %collective-permute-start.58 = (f32[10,128]{1,0:T(8,128)}, f32[10,128]{1,0:T(8,128)S(1)}, u32[]{:S(2)}, u32[]{:S(2)}) collective-permute-start(f32[10,128]{1,0:T(8,128)} %slice.437), channel_id=1, source_target_pairs={{0,1},{1,0},{2,3},{3,2},{4,5},{5,4},{6,7},{7,6},{8,9},{9,8},{10,11... | collective-permute-start | bytes 15368 | tf_op jit(solution)/shard_map/ppermute | solution.py:138
  463.7 5.6 collective-permute-start.59
  466.0 6.2 %collective-permute-start.60 = (f32[10,128]{1,0:T(8,128)}, f32[10,128]{1,0:T(8,128)}, u32[]{:S(2)}, u32[]{:S(2)}) collective-permute-start(f32[10,128]{1,0:T(8,128)} %slice.437), channel_id=1, source_target_pairs={{0,3},{1,2},{2,1},{3,0},{4,7},{5,6},{6,5},{7,4},{8,11},{9,10},{10,... | collective-permute-start | bytes 15368 | tf_op jit(solution)/shard_map/ppermute | solution.py:138
  469.2 11.3 %collective-permute-start.32 = (bf16[128,1024]{1,0:T(8,128)(2,1)}, bf16[128,1024]{1,0:T(8,128)(2,1)S(1)}, u32[]{:S(2)}, u32[]{:S(2)}) collective-permute-start(bf16[128,1024]{1,0:T(8,128)(2,1)} %get-tuple-element.766), channel_id=1, source_target_pairs={{0,1},{1,0},{2,3},{3,2},{4,5},{5,4},{6,7},{7,6},{8,9},{9,8},{10,11... | collective-permute-start | bytes 786440 | tf_op jit(solution)/shard_map/ppermute | solution.py:138
  469.3 21.5 %collective-permute-start.33 = (bf16[128,1024]{1,0:T(8,128)(2,1)}, bf16[128,1024]{1,0:T(8,128)(2,1)}, u32[]{:S(2)}, u32[]{:S(2)}) collective-permute-start(bf16[128,1024]{1,0:T(8,128)(2,1)} %get-tuple-element.768), channel_id=1, source_target_pairs={{0,2},{1,3},{2,0},{3,1},{4,6},{5,7},{6,4},{7,5},{8,10},{9,11},{10,... | collective-permute-start | bytes 786440 | tf_op jit(solution)/shard_map/ppermute | solution.py:138
  472.2 18.5 %collective-permute-start.34 = (bf16[128,1024]{1,0:T(8,128)(2,1)}, bf16[128,1024]{1,0:T(8,128)(2,1)}, u32[]{:S(2)}, u32[]{:S(2)}) collective-permute-start(bf16[128,1024]{1,0:T(8,128)(2,1)} %get-tuple-element.767), channel_id=1, source_target_pairs={{0,3},{1,2},{2,1},{3,0},{4,7},{5,6},{6,5},{7,4},{8,11},{9,10},{10,... | collective-permute-start | bytes 786440 | tf_op jit(solution)/shard_map/ppermute | solution.py:138
  493.6 6.5 %collective-permute-start.51 = (bf16[128,512]{0,1:T(8,128)(2,1)S(1)}, bf16[128,512]{0,1:T(8,128)(2,1)S(1)}, u32[]{:S(2)}, u32[]{:S(2)}) collective-permute-start(bf16[128,512]{0,1:T(8,128)(2,1)S(1)} %get-tuple-element.779), channel_id=1, source_target_pairs={{0,8},{4,12},{8,0},{12,4},{16,24},{20,28},{24,16},{28,20},{1,9},{5... | collective-permute-start | bytes 393224 | tf_op jit(solution)/shard_map/ppermute | solution.py:138
  494.2 10.7 %collective-permute-start.52 = (bf16[128,512]{0,1:T(8,128)(2,1)S(1)}, bf16[128,512]{0,1:T(8,128)(2,1)S(1)}, u32[]{:S(2)}, u32[]{:S(2)}) collective-permute-start(bf16[128,512]{0,1:T(8,128)(2,1)S(1)} %get-tuple-element.781), channel_id=1, source_target_pairs={{0,16},{4,20},{8,24},{12,28},{16,0},{20,4},{24,8},{28,12},{1,17},{... | collective-permute-start | bytes 393224 | tf_op jit(solution)/shard_map/ppermute | solution.py:138
  494.7 10.2 %collective-permute-start.53 = (bf16[128,512]{0,1:T(8,128)(2,1)S(1)}, bf16[128,512]{0,1:T(8,128)(2,1)S(1)}, u32[]{:S(2)}, u32[]{:S(2)}) collective-permute-start(bf16[128,512]{0,1:T(8,128)(2,1)S(1)} %get-tuple-element.780), channel_id=1, source_target_pairs={{0,24},{4,28},{8,16},{12,20},{16,8},{20,12},{24,0},{28,4},{1,25},{... | collective-permute-start | bytes 393224 | tf_op jit(solution)/shard_map/ppermute | solution.py:138
  499.0 10.0 %collective-permute-start.36 = (bf16[128,1408]{1,0:T(8,128)(2,1)S(1)}, bf16[128,1408]{1,0:T(8,128)(2,1)S(1)}, u32[]{:S(2)}, u32[]{:S(2)}) collective-permute-start(bf16[128,1408]{1,0:T(8,128)(2,1)S(1)} %get-tuple-element.763), channel_id=1, source_target_pairs={{0,8},{4,12},{8,0},{12,4},{16,24},{20,28},{24,16},{28,20},{1,9},{5... | collective-permute-start | bytes 1081352 | tf_op jit(solution)/shard_map/ppermute | solution.py:138
  499.6 13.6 %collective-permute-start.37 = (bf16[128,1408]{1,0:T(8,128)(2,1)S(1)}, bf16[128,1408]{1,0:T(8,128)(2,1)S(1)}, u32[]{:S(2)}, u32[]{:S(2)}) collective-permute-start(bf16[128,1408]{1,0:T(8,128)(2,1)S(1)} %get-tuple-element.765), channel_id=1, source_target_pairs={{0,16},{4,20},{8,24},{12,28},{16,0},{20,4},{24,8},{28,12},{1,17},{... | collective-permute-start | bytes 1081352 | tf_op jit(solution)/shard_map/ppermute | solution.py:138
  500.1 13.0 %collective-permute-start.38 = (bf16[128,1408]{1,0:T(8,128)(2,1)S(1)}, bf16[128,1408]{1,0:T(8,128)(2,1)S(1)}, u32[]{:S(2)}, u32[]{:S(2)}) collective-permute-start(bf16[128,1408]{1,0:T(8,128)(2,1)S(1)} %get-tuple-element.764), channel_id=1, source_target_pairs={{0,24},{4,28},{8,16},{12,20},{16,8},{20,12},{24,0},{28,4},{1,25},{... | collective-permute-start | bytes 1081352 | tf_op jit(solution)/shard_map/ppermute | solution.py:138
  516.0 9.5 %collective-permute-start.39 = (bf16[32,512]{1,0:T(8,128)(2,1)S(1)}, bf16[32,512]{1,0:T(8,128)(2,1)S(1)}, u32[]{:S(2)}, u32[]{:S(2)}) collective-permute-start(bf16[32,512]{1,0:T(8,128)(2,1)S(1)} %get-tuple-element.830), channel_id=1, source_target_pairs={{0,1},{1,0},{2,3},{3,2},{4,5},{5,4},{6,7},{7,6},{8,9},{9,8},{10,11... | collective-permute-start | bytes 98312 | tf_op jit(solution)/shard_map/ppermute | solution.py:138
  523.1 4.8 collective-permute-start.40
  523.9 5.8 %collective-permute-start.41 = (bf16[32,512]{1,0:T(8,128)(2,1)S(1)}, bf16[32,512]{1,0:T(8,128)(2,1)S(1)}, u32[]{:S(2)}, u32[]{:S(2)}) collective-permute-start(bf16[32,512]{1,0:T(8,128)(2,1)S(1)} %get-tuple-element.831), channel_id=1, source_target_pairs={{0,3},{1,2},{2,1},{3,0},{4,7},{5,6},{6,5},{7,4},{8,11},{9,10},{10,... | collective-permute-start | bytes 98312 | tf_op jit(solution)/shard_map/ppermute | solution.py:138
  529.8 6.4 %collective-permute-start.42 = (bf16[32,640]{1,0:T(8,128)(2,1)S(1)}, bf16[32,640]{1,0:T(8,128)(2,1)S(1)}, u32[]{:S(2)}, u32[]{:S(2)}) collective-permute-start(bf16[32,640]{1,0:T(8,128)(2,1)S(1)} %pad_maximum_fusion.26), channel_id=1, source_target_pairs={{0,1},{1,0},{2,3},{3,2},{4,5},{5,4},{6,7},{7,6},{8,9},{9,8},{10,11... | collective-permute-start | bytes 122888 | tf_op jit(solution)/shard_map/ppermute | solution.py:138
  531.1 5.3 collective-permute-start.43
  532.0 5.8 %collective-permute-start.44 = (bf16[32,640]{1,0:T(8,128)(2,1)S(1)}, bf16[32,640]{1,0:T(8,128)(2,1)S(1)}, u32[]{:S(2)}, u32[]{:S(2)}) collective-permute-start(bf16[32,640]{1,0:T(8,128)(2,1)S(1)} %pad_maximum_fusion.26), channel_id=1, source_target_pairs={{0,3},{1,2},{2,1},{3,0},{4,7},{5,6},{6,5},{7,4},{8,11},{9,10},{10,... | collective-permute-start | bytes 122888 | tf_op jit(solution)/shard_map/ppermute | solution.py:138
  538.0 5.4 collective-permute-start.46
  539.8 7.1 %collective-permute-start.47 = (bf16[128,640]{1,0:T(8,128)(2,1)S(1)}, bf16[128,640]{1,0:T(8,128)(2,1)S(1)}, u32[]{:S(2)}, u32[]{:S(2)}) collective-permute-start(bf16[128,640]{1,0:T(8,128)(2,1)S(1)} %get-tuple-element.818), channel_id=1, source_target_pairs={{0,16},{4,20},{8,24},{12,28},{16,0},{20,4},{24,8},{28,12},{1,17},{... | collective-permute-start | bytes 491528 | tf_op jit(solution)/shard_map/ppermute | solution.py:138
  540.1 6.7 %collective-permute-start.48 = (bf16[128,640]{1,0:T(8,128)(2,1)S(1)}, bf16[128,640]{1,0:T(8,128)(2,1)S(1)}, u32[]{:S(2)}, u32[]{:S(2)}) collective-permute-start(bf16[128,640]{1,0:T(8,128)(2,1)S(1)} %get-tuple-element.818), channel_id=1, source_target_pairs={{0,24},{4,28},{8,16},{12,20},{16,8},{20,12},{24,0},{28,4},{1,25},{... | collective-permute-start | bytes 491528 | tf_op jit(solution)/shard_map/ppermute | solution.py:138
  547.7 4.5 collective-permute-start.49
  549.5 1.7 collective-permute-start.45
  (91 other events, 902.5 us)
Sparse Core Ops, SparseCore 0:
  22.6 37.6 all-gather.1
  291.0 46.2 reduce-scatter.3
